TPU v7x, 512 devices: a whole 4x8x8 slice. The times are simulated.
512 devices in a mesh: rep: 32 (over z, y_hi, core), fsdp: 16 (over x, y_lo).
Axes of the slice: x: 4, y: 8 (y_hi: 2, y_lo: 4; y = y_hi * 4 + y_lo), z: 8, core: 2. Of those that a mesh axis runs over, the one named last changes fastest.
Arguments:
- tokens: bfloat16 [131072, 4096], P(('rep', 'fsdp')), may hold values from -6 to 6
- cotangent: bfloat16 [131072, 512], P(('rep', 'fsdp')), may hold values from -6 to 6
- norm_gain: float32 [4096], replicated, may hold values from 0.25 to 1.75
- local_weight: bfloat16 [32, 4096, 512], P('rep', 'fsdp'), may hold values from -0.1875 to 0.1875
- anchor_weight: bfloat16 [4096, 512], P('fsdp'), may hold values from -0.09375 to 0.09375
- outer_master: float32 [4096, 512], P(('fsdp', 'rep')), may hold values from -0.09375 to 0.09375
- outer_moment: float32 [4096, 512], P(('fsdp', 'rep')), may hold values from -0.06 to 0.06
Outputs:
- grad_weight: bfloat16 [32, 4096, 512], P('rep', 'fsdp')
- grad_tokens: bfloat16 [131072, 4096], P(('rep', 'fsdp'))
- synced_weight: bfloat16 [4096, 512], P('fsdp')
- new_master: float32 [4096, 512], P(('fsdp', 'rep'))
- new_moment: float32 [4096, 512], P(('fsdp', 'rep'))
All inputs are finite; a program needn't handle non-finite values.
Results may differ from a plain program's by a relative error of at most 0.03.
Values may be sent and summed in bfloat16 or wider, within the bound.
No kernel may reach another device: no remote copies, remote signals or barrier semaphores. Data moves between devices by JAX's collectives and lax.ppermute only.
A program may use at most 64 MiB of HBM per device.

v0:
```python
import jax
import jax.numpy as jnp
from jax import lax
from jax.sharding import PartitionSpec as P

scale_eps = 1e-06
code_range = 448.0
norm_eps = 1e-05
outer_mu = 0.9
outer_rate = 0.7


def quantize(values):
    blocks = values.reshape(values.shape[:-1] + (values.shape[-1] // 128, 128))
    peak = jnp.max(jnp.abs(blocks), axis=-1)
    scale = ((peak + scale_eps) / code_range).astype(jnp.bfloat16)
    codes = (blocks / scale.astype(jnp.float32)[..., None]).astype(jnp.bfloat16)
    return (codes.reshape(values.shape), scale)


def dequantize(codes, scale):
    blocks = codes.astype(jnp.float32).reshape(codes.shape[:-1] + (codes.shape[-1] // 128, 128))
    return (blocks * scale.astype(jnp.float32)[..., None]).reshape(codes.shape)


def local(tokens, cotangent, norm_gain, local_weight, anchor_weight, outer_master, outer_moment):
    key_width = cotangent.shape[1]
    weight = local_weight[0]
    own_rows = weight.shape[0]
    replicas = lax.axis_size("rep")
    xfull = tokens.astype(jnp.float32)
    inv = lax.rsqrt(jnp.mean(xfull * xfull, axis=-1, keepdims=True) + norm_eps)
    normed = (xfull * inv * norm_gain).astype(jnp.bfloat16)
    gathered = lax.dot_general(
        cotangent,
        lax.all_gather(weight, "fsdp", axis=0, tiled=True),
        (((1,), (1,)), ((), ())),
        preferred_element_type=jnp.float32,
    )
    grad_low = lax.optimization_barrier(gathered.astype(jnp.bfloat16))
    summed = lax.psum_scatter(
        lax.dot_general(
            normed, cotangent, (((0,), (0,)), ((), ())), preferred_element_type=jnp.float32
        ).astype(jnp.bfloat16),
        "fsdp",
        scatter_dimension=0,
        tiled=True,
    )
    grad_normed = grad_low.astype(jnp.float32)
    scaled = grad_normed * norm_gain
    grad_in = inv * scaled - xfull * inv * inv * inv * jnp.mean(
        xfull * scaled, axis=-1, keepdims=True
    )
    grad_tokens = grad_in.astype(jnp.bfloat16)
    anchor_full = anchor_weight.astype(jnp.float32)
    delta = anchor_full - weight.astype(jnp.float32)
    codes, scale = quantize(delta)
    slab = own_rows // replicas
    codes_in, scale_in = (
        lax.all_to_all(
            codes.reshape(replicas, slab, key_width), "rep", split_axis=0, concat_axis=0, tiled=True
        ),
        lax.all_to_all(
            scale.reshape(replicas, slab, key_width // 128),
            "rep",
            split_axis=0,
            concat_axis=0,
            tiled=True,
        ),
    )
    pseudo = jnp.sum(dequantize(codes_in, scale_in), axis=0) / replicas
    new_moment = outer_mu * outer_moment + pseudo
    step = outer_rate * (pseudo + outer_mu * new_moment)
    new_master = outer_master - step
    step_codes, step_scale = quantize(step)
    all_codes, all_scale = (
        lax.all_gather(step_codes, "rep", axis=0, tiled=True),
        lax.all_gather(step_scale, "rep", axis=0, tiled=True),
    )
    synced_weight = (anchor_full - dequantize(all_codes, all_scale)).astype(jnp.bfloat16)
    return (summed[None], grad_tokens, synced_weight, new_master, new_moment)


def solution(mesh):
    in_specs = (
        P(("rep", "fsdp"), None),
        P(("rep", "fsdp"), None),
        P(),
        P("rep", "fsdp", None),
        P("fsdp", None),
        P(("fsdp", "rep"), None),
        P(("fsdp", "rep"), None),
    )
    out_specs = (
        P("rep", "fsdp", None),
        P(("rep", "fsdp"), None),
        P("fsdp", None),
        P(("fsdp", "rep"), None),
        P(("fsdp", "rep"), None),
    )
    return jax.shard_map(local, mesh=mesh, in_specs=in_specs, out_specs=out_specs, check_vma=False)
```

profile of v0, /device:TPU:13, one launch (start us, length us, event | category | flops | bytes accessed | tf_op | source)
XLA Modules:
  0.0 297.2 jit_solution(241395526202381228)
XLA Ops:
  7.2 0.7 all-gather.4.cloned.1.call-update
  8.0 107.0 %all-gather.4.cloned.1.call-done = bf16[1,4096,512]{2,1,0:T(8,128)(2,1)} async-done(((bf16[1,256,512]{2,1,0:T(8,128)(2,1)}), bf16[1,4096,512]{2,1,0:T(8,128)(2,1)}) %all-gather.4.cloned.1.call-update) | async-done | bytes 4194320 | tf_op jit(solution)/shard_map/all_gather | solution.py:36
  115.0 3.6 %convolution_convert_fusion.1 = bf16[256,4096]{1,0:T(8,128)(2,1)S(1)} fusion(bf16[256,512]{1,0:T(8,128)(2,1)S(1)} %copy-done, bf16[1,4096,512]{2,1,0:T(8,128)(2,1)} %all-gather.4.cloned.1.call-done), kind=kOutput, calls=%fused_computation.4 | convolution fusion | flops 1074790400 | bytes 6553600 | tf_op jit(solution)/shard_map/dot_general | solution.py:34
  118.6 1.5 fusion.8
  120.2 0.6 copy-done.6
  120.8 3.4 %convolution_convert_fusion = bf16[4096,512]{1,0:T(8,128)(2,1)} fusion(bf16[256,512]{1,0:T(8,128)(2,1)S(1)} %copy-done, bf16[256,4096]{1,0:T(8,128)(2,1)S(1)} %copy-done.1, f32[4096]{0:T(1024)S(1)} %copy-done.5, f32[256]{0:T(256)S(1)} %add_rsqrt_fusion), kind=kOutput, calls=%fused_computation.3 | convolution fusion | flops 1080033280 | bytes 6571008 | tf_op jit(solution)/shard_map/dot_general | solution.py:42
  124.2 0.9 copy-done.2
  125.2 0.9 fusion.16
  126.1 1.2 abs.13
  127.3 0.3 reduce_max.18
  127.8 0.1 convert_element_type.91
  127.9 0.6 copy.22
  128.5 12.5 %all-to-all-start.1 = ((bf16[32,8,4]{1,2,0:T(4,128)(2,1)}), bf16[32,8,4]{1,2,0:T(4,128)(2,1)}, u32[]{:S(2)}, u32[]{:S(2)}) async-start(bf16[32,8,4]{1,2,0:T(4,128)(2,1)} %copy.22), calls=%async_computation.2 | async-start | bytes 65536 | tf_op jit(solution)/shard_map/all_to_all | solution.py:63
  141.0 0.1 copy.21
  141.1 0.3 div.50
  141.5 1.0 div.51
  142.5 1.9 fusion.15
  144.3 9.0 %all-to-all-done.1 = bf16[32,8,4]{1,2,0:T(4,128)(2,1)} async-done(((bf16[32,8,4]{1,2,0:T(4,128)(2,1)}), bf16[32,8,4]{1,2,0:T(4,128)(2,1)}, u32[]{:S(2)}, u32[]{:S(2)}) %all-to-all-start.1) | async-done | bytes 2080 | tf_op jit(solution)/shard_map/all_to_all | solution.py:63
  153.3 3.8 %all-to-all-start = ((bf16[32,8,512]{2,1,0:T(8,128)(2,1)}), bf16[32,8,512]{2,1,0:T(8,128)(2,1)S(1)}, u32[]{:S(2)}, u32[]{:S(2)}) async-start(bf16[32,8,512]{2,1,0:T(8,128)(2,1)} %fusion.15), calls=%async_computation.1 | async-start | bytes 524288 | tf_op jit(solution)/shard_map/all_to_all | solution.py:60
  157.1 0.8 convert_element_type.92
  157.9 20.3 %all-to-all-done = bf16[32,8,512]{2,1,0:T(8,128)(2,1)S(1)} async-done(((bf16[32,8,512]{2,1,0:T(8,128)(2,1)}), bf16[32,8,512]{2,1,0:T(8,128)(2,1)S(1)}, u32[]{:S(2)}, u32[]{:S(2)}) %all-to-all-start) | async-done | bytes 262176 | tf_op jit(solution)/shard_map/all_to_all | solution.py:60
  178.1 0.2 fusion.14
  178.3 1.4 fusion.20
  179.7 0.1 bitcast_reduce_fusion
  179.8 53.5 %all-gather.1 = bf16[32,8,4]{1,2,0:T(4,128)(2,1)S(1)} all-gather(bf16[1,8,4]{1,2,0:T(4,128)(2,1)S(1)} %get-tuple-element.10), channel_id=1, replica_groups=mesh['rep'=32,'fsdp'=16] {'rep'}, dimensions={0}, use_global_device_ids=true | all-gather | bytes 2112 | tf_op jit(solution)/shard_map/all_gather | solution.py:78
  233.3 0.1 copy.23
  233.4 0.2 copy.26
  233.6 0.1 fusion.17
  233.6 51.1 %all_gather.10 = bf16[256,512]{1,0:T(8,128)(2,1)S(1)} all-gather(bf16[8,512]{1,0:T(8,128)(2,1)S(1)} %fusion.17), channel_id=1, replica_groups=mesh['rep'=32,'fsdp'=16] {'rep'}, dimensions={0}, use_global_device_ids=true | all-gather | bytes 270336 | tf_op jit(solution)/shard_map/all_gather | solution.py:77
  284.7 0.3 mul.111
  285.0 0.8 fusion.13
  285.9 4.4 %fusion.6 = bf16[256,4096]{1,0:T(8,128)(2,1)} fusion(bf16[256,4096]{1,0:T(8,128)(2,1)} %param.7, bf16[256,4096]{1,0:T(8,128)(2,1)S(1)} %convolution_convert_fusion.1, f32[256]{0:T(256)S(1)} %broadcast_multiply_fusion, f32[4096]{0:T(1024)S(1)} %copy-done.5, f32[256]{0:T(256)S(1)} %copy-done.7), kind=kLoop, calls=%fused_computation.11 | loop fusion | flops 10485760 | bytes 6309888 | tf_op jit(solution)/shard_map/convert_element_type | solution.py:54
  (25 shorter events, 0.3 us)
Async XLA Ops:
  7.2 107.8 %copy-start = (bf16[256,512]{1,0:T(8,128)(2,1)S(1)}, bf16[256,512]{1,0:T(8,128)(2,1)}, u32[]{:S(2)}) copy-start(bf16[256,512]{1,0:T(8,128)(2,1)} %param.8) | copy-start | bytes 786436
  7.2 111.4 %copy-start.5 = (f32[4096]{0:T(1024)S(1)}, f32[4096]{0:T(1024)}, u32[]{:S(2)}) copy-start(f32[4096]{0:T(1024)} %param.9) | copy-start | bytes 49156
  7.2 107.8 %all-gather.4.cloned.1.call-start = ((), (), s32[]{:S(2)}) async-start(), calls=%async_computation.4 | async-start | bytes 4456448 | tf_op jit(solution)/shard_map/all_gather | solution.py:36
  7.9 282.4 %reduce-scatter.2.cloned.1.call-start = ((), (), s32[]{:S(2)}) async-start(), calls=%async_computation.3 | async-start | bytes 4456448 | tf_op jit(solution)/shard_map/reduce_scatter | solution.py:41
  115.0 3.6 %copy-start.1 = (bf16[256,4096]{1,0:T(8,128)(2,1)S(1)}, bf16[256,4096]{1,0:T(8,128)(2,1)}, u32[]{:S(2)}) copy-start(bf16[256,4096]{1,0:T(8,128)(2,1)} %param.7) | copy-start | bytes 6291460
  120.2 0.6 copy-start.6
  124.2 0.9 copy-start.2
  124.2 1.0 copy-start.3
  128.5 24.8 %all-to-all-start.1 = ((bf16[32,8,4]{1,2,0:T(4,128)(2,1)}), bf16[32,8,4]{1,2,0:T(4,128)(2,1)}, u32[]{:S(2)}, u32[]{:S(2)}) async-start(bf16[32,8,4]{1,2,0:T(4,128)(2,1)} %copy.22), calls=%async_computation.2 | async-start | bytes 65536 | tf_op jit(solution)/shard_map/all_to_all | solution.py:63
  141.4 144.4 %copy-start.8 = (f32[256]{0:T(256)S(1)}, f32[256]{0:T(256)}, u32[]{:S(2)}) copy-start(f32[256]{0:T(256)} %get-tuple-element.5) | copy-start | bytes 3076
  141.5 144.4 %copy-start.7 = (f32[256]{0:T(256)S(1)}, f32[256]{0:T(256)}, u32[]{:S(2)}) copy-start(f32[256]{0:T(256)} %copy-done.6) | copy-start | bytes 3076
  153.3 24.9 %all-to-all-start = ((bf16[32,8,512]{2,1,0:T(8,128)(2,1)}), bf16[32,8,512]{2,1,0:T(8,128)(2,1)S(1)}, u32[]{:S(2)}, u32[]{:S(2)}) async-start(bf16[32,8,512]{2,1,0:T(8,128)(2,1)} %fusion.15), calls=%async_computation.1 | async-start | bytes 524288 | tf_op jit(solution)/shard_map/all_to_all | solution.py:60
  179.7 110.6 %copy-start.4 = (f32[8,512]{1,0:T(8,128)}, f32[8,512]{1,0:T(8,128)S(1)}, u32[]{:S(2)}) copy-start(f32[8,512]{1,0:T(8,128)S(1)} %get-tuple-element.8) | copy-start | bytes 49156
Sparse Core Ops, SparseCore 0:
  10.1 104.8 all-gather.3
  124.4 109.0 reduce-scatter.1
where the time goes:
time: 298 us; the launch traced here: 297 us
  waiting for transfers between devices  137 us (46%)
  blocking collectives  105 us (35%)
  starting transfers between devices  16.4 us (6%)
  between operations  14.2 us (5%)
  other arithmetic  12.4 us (4%)
  matrix products  7.07 us (2%)
  local copies, waits for them, and re-layouts  5.67 us (2%)
    all_gather x1, waiting for transfers between devices, local(): lax.all_gather(weight, 'fsdp', axis=0, tiled=True)  107 us
    all_gather x1, blocking collectives, local(): lax.all_gather(step_scale, 'rep', axis=0, tiled=True)  53.5 us
    all_gather x1, blocking collectives, local(): lax.all_gather(step_codes, 'rep', axis=0, tiled=True)  51.1 us
    all_to_all x1, waiting for transfers between devices, local(): lax.all_to_all(codes.reshape(replicas, slab, key_width), 'rep', split_axi...  20.3 us
    all_to_all x1, starting transfers between devices, local(): lax.all_to_all(scale.reshape(replicas, slab, key_width // 128), 'rep', sp...  12.5 us
    all_to_all x1, waiting for transfers between devices, local(): lax.all_to_all(scale.reshape(replicas, slab, key_width // 128), 'rep', sp...  8.96 us
  transfers between devices with their start and end apart: 4, of which 3 were waited for; matrix products, arithmetic and copies ran while one was open for 5% of the time, Pallas kernels for 0%

commit v1 on v0

v1 whole, which is shorter than its diff:
```python
import functools

import jax
import jax.numpy as jnp
from jax import lax
from jax.experimental import pallas as pl
from jax.experimental.pallas import tpu as pltpu
from jax.sharding import PartitionSpec as P

scale_eps = 1e-06
code_range = 448.0
norm_eps = 1e-05
outer_mu = 0.9
outer_rate = 0.7

SIDE = 4
ROWS = 32
F32 = jnp.float32
BF16 = jnp.bfloat16
PARAMS = pltpu.CompilerParams(vmem_limit_bytes=48 * 1024 * 1024)


def coords():
    index = lax.axis_index("fsdp")
    return index // SIDE, index % SIDE


def along_x(k):
    return [(x * SIDE + y, (x + k) % SIDE * SIDE + y) for x in range(SIDE) for y in range(SIDE)]


def along_y(k):
    return [(x * SIDE + y, x * SIDE + (y + k) % SIDE) for x in range(SIDE) for y in range(SIDE)]


def columns(step, width):
    return pl.ds(pl.multiple_of(step % SIDE * width, width), width)


def norm_kernel(tokens, gain, inv_out, *normed_out):
    x, _ = coords()
    width = normed_out[0].shape[1]
    full = tokens[...].astype(F32)
    inv = lax.rsqrt(jnp.mean(full * full, axis=-1, keepdims=True) + norm_eps)
    inv_out[...] = jnp.broadcast_to(inv, inv_out.shape)
    for k, out in enumerate(normed_out):
        cols = columns(x + k, width)
        out[...] = (tokens[:, cols].astype(F32) * inv * gain[:, cols]).astype(BF16)


def norm(tokens, gain):
    count, width = tokens.shape
    part = width // SIDE
    return pl.pallas_call(
        norm_kernel,
        grid=(count // ROWS,),
        in_specs=[pl.BlockSpec((ROWS, width), lambda i: (i, 0)), pl.BlockSpec((1, width), lambda i: (0, 0))],
        out_specs=[pl.BlockSpec((ROWS, 128), lambda i: (i, 0))]
        + [pl.BlockSpec((ROWS, part), lambda i: (i, 0))] * SIDE,
        out_shape=[jax.ShapeDtypeStruct((count, 128), F32)]
        + [jax.ShapeDtypeStruct((count, part), BF16)] * SIDE,
        compiler_params=PARAMS,
        cost_estimate=pl.CostEstimate(flops=4 * count * width, bytes_accessed=4 * count * width, transcendentals=0),
        name="norm",
    )(tokens, gain)


def back_kernel(*refs):
    cots, weights, outs = refs[:SIDE], refs[SIDE : 2 * SIDE], refs[2 * SIDE :]
    _, y = coords()
    rows = weights[0].shape[0]
    for j in range(SIDE):
        cols = columns(y - j + SIDE, rows)
        weight = weights[j][...]
        for k in range(SIDE):
            outs[k][:, cols] = lax.dot_general(
                cots[k][...], weight, (((1,), (1,)), ((), ())), preferred_element_type=F32
            ).astype(BF16)


def back(cots, weights):
    count, width = cots[0].shape
    rows = weights[0].shape[0]
    flops = 2 * SIDE * SIDE * count * rows * width
    return pl.pallas_call(
        back_kernel,
        out_shape=[jax.ShapeDtypeStruct((count, SIDE * rows), BF16)] * SIDE,
        compiler_params=PARAMS,
        cost_estimate=pl.CostEstimate(flops=flops, bytes_accessed=4 << 20, transcendentals=0),
        name="back",
    )(*cots, *weights)


def partial_kernel(*refs):
    normed, cots, outs = refs[:SIDE], refs[SIDE : 2 * SIDE], refs[2 * SIDE :]
    _, y = coords()
    rows = outs[0].shape[0]
    for j in range(SIDE):
        cols = columns(y + j, rows)
        total = jnp.zeros(outs[0].shape, F32)
        for k in range(SIDE):
            total = total + lax.dot_general(
                normed[k][:, cols], cots[k][...], (((0,), (0,)), ((), ())), preferred_element_type=F32
            )
        outs[j][...] = total.astype(outs[j].dtype)


def partial(normed, cots):
    count, width = cots[0].shape
    rows = normed[0].shape[1] // SIDE
    flops = 2 * SIDE * SIDE * count * rows * width
    return pl.pallas_call(
        partial_kernel,
        out_shape=[jax.ShapeDtypeStruct((rows, width), F32)]
        + [jax.ShapeDtypeStruct((rows, width), BF16)] * (SIDE - 1),
        compiler_params=PARAMS,
        cost_estimate=pl.CostEstimate(flops=flops, bytes_accessed=5 << 20, transcendentals=0),
        name="partial",
    )(*normed, *cots)


def finish_kernel(tokens, gain, inv_in, *refs):
    pieces, out = refs[:SIDE], refs[SIDE]
    x, _ = coords()
    width = pieces[0].shape[1]
    inv = inv_in[:, :1]
    total = jnp.zeros(inv.shape, F32)
    for k, piece in enumerate(pieces):
        cols = columns(x - k + SIDE, width)
        scaled = piece[...].astype(F32) * gain[:, cols]
        total = total + jnp.sum(tokens[:, cols].astype(F32) * scaled, axis=-1, keepdims=True)
    factor = inv * inv * inv * (total / (SIDE * width))
    for k, piece in enumerate(pieces):
        cols = columns(x - k + SIDE, width)
        scaled = piece[...].astype(F32) * gain[:, cols]
        out[:, cols] = (inv * scaled - tokens[:, cols].astype(F32) * factor).astype(BF16)


def finish(tokens, gain, inv, pieces):
    count, width = tokens.shape
    part = width // SIDE
    return pl.pallas_call(
        finish_kernel,
        grid=(count // ROWS,),
        in_specs=[
            pl.BlockSpec((ROWS, width), lambda i: (i, 0)),
            pl.BlockSpec((1, width), lambda i: (0, 0)),
            pl.BlockSpec((ROWS, 128), lambda i: (i, 0)),
        ]
        + [pl.BlockSpec((ROWS, part), lambda i: (i, 0))] * SIDE,
        out_specs=pl.BlockSpec((ROWS, width), lambda i: (i, 0)),
        out_shape=jax.ShapeDtypeStruct((count, width), BF16),
        compiler_params=PARAMS,
        cost_estimate=pl.CostEstimate(flops=6 * count * width, bytes_accessed=6 * count * width, transcendentals=0),
        name="finish",
    )(tokens, gain, inv, *pieces)


def requantized(values):
    parts = []
    for start in range(0, values.shape[-1], 128):
        block = values[..., start : start + 128]
        peak = jnp.max(jnp.abs(block), axis=-1, keepdims=True)
        scale = ((peak + scale_eps) / code_range).astype(BF16).astype(F32)
        parts.append((block / scale).astype(BF16).astype(F32) * scale)
    return jnp.concatenate(parts, axis=-1)


def outer_kernel(replicas, local, anchor, master, moment, master_out, moment_out, synced_out):
    slab = anchor.shape[0]
    start = anchor[...]
    total = jnp.zeros(start.shape, F32)
    held = local[...].astype(F32)
    for r in range(replicas):
        total = total + requantized(start - held[r * slab : (r + 1) * slab])
    pseudo = total / replicas
    new_moment = outer_mu * moment[...] + pseudo
    step = outer_rate * (pseudo + outer_mu * new_moment)
    moment_out[...] = new_moment
    master_out[...] = master[...] - step
    synced = start - requantized(step)
    synced_out[...] = jnp.concatenate([synced] * replicas, axis=0).astype(BF16)


def outer(local, anchor, master, moment, replicas):
    slab, width = master.shape
    return pl.pallas_call(
        functools.partial(outer_kernel, replicas),
        out_shape=[
            jax.ShapeDtypeStruct((slab, width), F32),
            jax.ShapeDtypeStruct((slab, width), F32),
            jax.ShapeDtypeStruct((slab * replicas, width), BF16),
        ],
        compiler_params=PARAMS,
        cost_estimate=pl.CostEstimate(
            flops=20 * replicas * slab * width, bytes_accessed=4 * replicas * slab * width, transcendentals=0
        ),
        name="outer",
    )(local, anchor, master, moment)


def local(tokens, cotangent, norm_gain, local_weight, anchor_weight, outer_master, outer_moment):
    key_width = cotangent.shape[1]
    weight = local_weight[0]
    own_rows = weight.shape[0]
    replicas = lax.axis_size("rep")
    slab = own_rows // replicas
    gain = norm_gain[None]

    def exchange(block):
        split = block.reshape(replicas, slab, key_width)
        return lax.all_to_all(split, "rep", split_axis=0, concat_axis=0, tiled=True).reshape(own_rows, key_width)

    gathered = exchange(weight)
    weights = [weight] + [lax.ppermute(weight, "fsdp", along_y(j)) for j in range(1, SIDE)]
    cots = [cotangent] + [lax.ppermute(cotangent, "fsdp", along_x(k)) for k in range(1, SIDE)]
    inv, *normed = norm(tokens, gain)
    normed = [normed[0]] + [lax.ppermute(normed[k], "fsdp", along_x(k)) for k in range(1, SIDE)]

    pieces = back([cots[(SIDE - k) % SIDE] for k in range(SIDE)], weights)
    pieces = [pieces[0]] + [lax.ppermute(pieces[k], "fsdp", along_x(k)) for k in range(1, SIDE)]

    parts = partial(normed, cots)
    grad_weight = parts[0]
    for j in range(1, SIDE):
        grad_weight = grad_weight + lax.ppermute(parts[j], "fsdp", along_y(j)).astype(F32)

    anchor_rows = lax.dynamic_slice_in_dim(anchor_weight, lax.axis_index("rep") * slab, slab, 0).astype(F32)
    new_master, new_moment, synced = outer(gathered, anchor_rows, outer_master, outer_moment, replicas)
    synced_weight = exchange(synced)

    grad_tokens = finish(tokens, gain, inv, pieces)
    return (grad_weight.astype(BF16)[None], grad_tokens, synced_weight, new_master, new_moment)


def solution(mesh):
    in_specs = (
        P(("rep", "fsdp"), None),
        P(("rep", "fsdp"), None),
        P(),
        P("rep", "fsdp", None),
        P("fsdp", None),
        P(("fsdp", "rep"), None),
        P(("fsdp", "rep"), None),
    )
    out_specs = (
        P("rep", "fsdp", None),
        P(("rep", "fsdp"), None),
        P("fsdp", None),
        P(("fsdp", "rep"), None),
        P(("fsdp", "rep"), None),
    )
    return jax.shard_map(local, mesh=mesh, in_specs=in_specs, out_specs=out_specs, check_vma=False)
```

time: 298 us -> 126 us (0.42)
  the two profiles are of different devices: /device:TPU:13 before, /device:TPU:8 now
where the time goes in v1:
time: 126 us; the launch traced here: 125 us
  starting transfers between devices  79.1 us (63%)
  Pallas kernels  17.3 us (14%)
  local copies, waits for them, and re-layouts  16 us (13%)
  waiting for transfers between devices  8.02 us (6%)
  other arithmetic  3.26 us (3%)
    all_to_all x2, starting transfers between devices, exchange(): lax.all_to_all(split, 'rep', split_axis=0, concat_axis=0, tiled=True)  26.3 us
    unnamed x49, local copies, waits for them, and re-layouts  16 us
    ppermute x3, starting transfers between devices, local(): lax.ppermute(cotangent, 'fsdp', along_x(k))  11.4 us
    ppermute x3, starting transfers between devices, local(): lax.ppermute(normed[k], 'fsdp', along_x(k))  11.3 us
    ppermute x3, starting transfers between devices, local(): lax.ppermute(parts[j], 'fsdp', along_y(j)).astype(F32)  11.1 us
    ppermute x3, starting transfers between devices, local(): lax.ppermute(weight, 'fsdp', along_y(j))  10.6 us
    ppermute x3, starting transfers between devices, local(): lax.ppermute(pieces[k], 'fsdp', along_x(k))  8.4 us
    all_to_all x2, waiting for transfers between devices, exchange(): lax.all_to_all(split, 'rep', split_axis=0, concat_axis=0, tiled=True)  7.98 us
  transfers between devices with their start and end apart: 17, of which 1 were waited for; matrix products, arithmetic and copies ran while one was open for 3% of the time, Pallas kernels for 14%

profile of v1, /device:TPU:8, one launch (start us, length us, event | category | flops | bytes accessed | tf_op | source)
XLA Modules:
  0.0 124.6 jit_solution(2388951052991234250)
XLA Ops:
  0.6 3.4 %collective-permute-start.3 = (bf16[256,512]{1,0:T(8,128)(2,1)}, bf16[256,512]{1,0:T(8,128)(2,1)S(1)}, u32[]{:S(2)}, u32[]{:S(2)}) collective-permute-start(bf16[256,512]{1,0:T(8,128)(2,1)} %refs_0_.1), channel_id=1, source_target_pairs={{0,4},{1,5},{2,6},{3,7},{4,8},{5,9},{6,10},{7,11},{8,12},{9,13},{1... | collective-permute-start | bytes 786440 | tf_op jit(solution)/shard_map/ppermute | solution.py:216
  4.0 4.6 %collective-permute-start.4 = (bf16[256,512]{1,0:T(8,128)(2,1)}, bf16[256,512]{1,0:T(8,128)(2,1)S(1)}, u32[]{:S(2)}, u32[]{:S(2)}) collective-permute-start(bf16[256,512]{1,0:T(8,128)(2,1)} %refs_0_.1), channel_id=1, source_target_pairs={{0,8},{1,9},{2,10},{3,11},{4,12},{5,13},{6,14},{7,15},{8,0},{9,1},... | collective-permute-start | bytes 786440 | tf_op jit(solution)/shard_map/ppermute | solution.py:216
  8.7 3.3 %collective-permute-start.5 = (bf16[256,512]{1,0:T(8,128)(2,1)}, bf16[256,512]{1,0:T(8,128)(2,1)S(1)}, u32[]{:S(2)}, u32[]{:S(2)}) collective-permute-start(bf16[256,512]{1,0:T(8,128)(2,1)} %refs_0_.1), channel_id=1, source_target_pairs={{0,12},{1,13},{2,14},{3,15},{4,0},{5,1},{6,2},{7,3},{8,4},{9,5},{1... | collective-permute-start | bytes 786440 | tf_op jit(solution)/shard_map/ppermute | solution.py:216
  12.0 4.5 %collective-permute-start.10 = (bf16[256,512]{1,0:T(8,128)(2,1)}, bf16[256,512]{1,0:T(8,128)(2,1)S(1)}, u32[]{:S(2)}, u32[]{:S(2)}) collective-permute-start(bf16[256,512]{1,0:T(8,128)(2,1)} %bitcast.2.refs_4_), channel_id=1, source_target_pairs={{0,2},{1,3},{2,0},{3,1},{4,6},{5,7},{6,4},{7,5},{8,10},{9,11},{10,... | collective-permute-start | bytes 786440 | tf_op jit(solution)/shard_map/ppermute | solution.py:215
  16.5 2.8 %collective-permute-start.11 = (bf16[256,512]{1,0:T(8,128)(2,1)}, bf16[256,512]{1,0:T(8,128)(2,1)S(1)}, u32[]{:S(2)}, u32[]{:S(2)}) collective-permute-start(bf16[256,512]{1,0:T(8,128)(2,1)} %bitcast.2.refs_4_), channel_id=1, source_target_pairs={{0,3},{1,0},{2,1},{3,2},{4,7},{5,4},{6,5},{7,6},{8,11},{9,8},{10,9... | collective-permute-start | bytes 786440 | tf_op jit(solution)/shard_map/ppermute | solution.py:215
  19.3 3.4 %collective-permute-start.9 = (bf16[256,512]{1,0:T(8,128)(2,1)}, bf16[256,512]{1,0:T(8,128)(2,1)S(1)}, u32[]{:S(2)}, u32[]{:S(2)}) collective-permute-start(bf16[256,512]{1,0:T(8,128)(2,1)} %bitcast.2.refs_4_), channel_id=1, source_target_pairs={{0,1},{1,2},{2,3},{3,0},{4,5},{5,6},{6,7},{7,4},{8,9},{9,10},{10,1... | collective-permute-start | bytes 786440 | tf_op jit(solution)/shard_map/ppermute | solution.py:215
  22.7 1.6 %copy-done = bf16[256,4096]{1,0:T(8,128)(2,1)S(1)} copy-done((bf16[256,4096]{1,0:T(8,128)(2,1)S(1)}, bf16[256,4096]{1,0:T(8,128)(2,1)}, u32[]{:S(2)}) %copy-start) | copy-done | bytes 2097176
  25.0 3.4 %norm.1 = (f32[256,128]{1,0:T(8,128)S(1)}, bf16[256,1024]{1,0:T(8,128)(2,1)S(1)}, bf16[256,1024]{1,0:T(8,128)(2,1)}, bf16[256,1024]{1,0:T(8,128)(2,1)S(1)}, bf16[256,1024]{1,0:T(8,128)(2,1)S(1)}) custom-call(bf16[256,4096]{1,0:T(8,128)(2,1)S(1)} %copy-done, f32[1,4096]{1,0:T(1,128)S(1)} %bitcast.10), custom_call_target="tpu_custom_call" | custom-call | flops 4194304 | bytes 4194304 | tf_op jit(solution)/shard_map/norm/pallas_call | solution.py:54
  29.2 2.8 %collective-permute-start = (bf16[256,1024]{1,0:T(8,128)(2,1)}, bf16[256,1024]{1,0:T(8,128)(2,1)S(1)}, u32[]{:S(2)}, u32[]{:S(2)}) collective-permute-start(bf16[256,1024]{1,0:T(8,128)(2,1)} %get-tuple-element.22), channel_id=1, source_target_pairs={{0,4},{1,5},{2,6},{3,7},{4,8},{5,9},{6,10},{7,11},{8,12},{9,13},{1... | collective-permute-start | bytes 1572872 | tf_op jit(solution)/shard_map/ppermute | solution.py:218
  32.0 4.0 %collective-permute-start.1 = (bf16[256,1024]{1,0:T(8,128)(2,1)S(1)}, bf16[256,1024]{1,0:T(8,128)(2,1)S(1)}, u32[]{:S(2)}, u32[]{:S(2)}) collective-permute-start(bf16[256,1024]{1,0:T(8,128)(2,1)S(1)} %get-tuple-element.23), channel_id=1, source_target_pairs={{0,8},{1,9},{2,10},{3,11},{4,12},{5,13},{6,14},{7,15},{8,0},{9,1},... | collective-permute-start | bytes 1572872 | tf_op jit(solution)/shard_map/ppermute | solution.py:218
  36.0 4.5 %collective-permute-start.2 = (bf16[256,1024]{1,0:T(8,128)(2,1)S(1)}, bf16[256,1024]{1,0:T(8,128)(2,1)}, u32[]{:S(2)}, u32[]{:S(2)}) collective-permute-start(bf16[256,1024]{1,0:T(8,128)(2,1)S(1)} %get-tuple-element.24), channel_id=1, source_target_pairs={{0,12},{1,13},{2,14},{3,15},{4,0},{5,1},{6,2},{7,3},{8,4},{9,5},{1... | collective-permute-start | bytes 1572872 | tf_op jit(solution)/shard_map/ppermute | solution.py:218
  40.6 3.3 %back.1 = (bf16[256,1024]{1,0:T(8,128)(2,1)S(1)}, bf16[256,1024]{1,0:T(8,128)(2,1)}, bf16[256,1024]{1,0:T(8,128)(2,1)}, bf16[256,1024]{1,0:T(8,128)(2,1)}) custom-call(bf16[256,512]{1,0:T(8,128)(2,1)S(1)} %copy-done.16, bf16[256,512]{1,0:T(8,128)(2,1)S(1)} %collective-permute-done.5.refs_7_.refs_1_, ...), custom_call_target="tpu_custom_call" | custom-call | flops 1073741824 | bytes 4194304 | tf_op jit(solution)/shard_map/back/pallas_call | solution.py:85
  43.8 1.9 %collective-permute-start.12 = (bf16[256,1024]{1,0:T(8,128)(2,1)}, bf16[256,1024]{1,0:T(8,128)(2,1)S(1)}, u32[]{:S(2)}, u32[]{:S(2)}) collective-permute-start(bf16[256,1024]{1,0:T(8,128)(2,1)} %get-tuple-element.31), channel_id=1, source_target_pairs={{0,4},{1,5},{2,6},{3,7},{4,8},{5,9},{6,10},{7,11},{8,12},{9,13},{1... | collective-permute-start | bytes 1572872 | tf_op jit(solution)/shard_map/ppermute | solution.py:221
  45.8 14.1 %all-to-all-start = ((bf16[32,8,512]{2,1,0:T(8,128)(2,1)}), bf16[32,8,512]{2,1,0:T(8,128)(2,1)S(1)}, u32[]{:S(2)}, u32[]{:S(2)}) async-start(bf16[32,8,512]{2,1,0:T(8,128)(2,1)} %bitcast.3), calls=%async_computation | async-start | bytes 524288 | tf_op jit(solution)/shard_map/all_to_all | solution.py:212
  59.9 3.1 %collective-permute-start.13 = (bf16[256,1024]{1,0:T(8,128)(2,1)}, bf16[256,1024]{1,0:T(8,128)(2,1)}, u32[]{:S(2)}, u32[]{:S(2)}) collective-permute-start(bf16[256,1024]{1,0:T(8,128)(2,1)} %get-tuple-element.32), channel_id=1, source_target_pairs={{0,8},{1,9},{2,10},{3,11},{4,12},{5,13},{6,14},{7,15},{8,0},{9,1},... | collective-permute-start | bytes 1572872 | tf_op jit(solution)/shard_map/ppermute | solution.py:221
  63.8 3.4 %collective-permute-start.14 = (bf16[256,1024]{1,0:T(8,128)(2,1)}, bf16[256,1024]{1,0:T(8,128)(2,1)}, u32[]{:S(2)}, u32[]{:S(2)}) collective-permute-start(bf16[256,1024]{1,0:T(8,128)(2,1)} %get-tuple-element.33), channel_id=1, source_target_pairs={{0,12},{1,13},{2,14},{3,15},{4,0},{5,1},{6,2},{7,3},{8,4},{9,5},{1... | collective-permute-start | bytes 1572872 | tf_op jit(solution)/shard_map/ppermute | solution.py:221
  68.1 1.0 copy-done.11
  69.1 1.0 copy-done.13
  70.1 1.0 copy-done.15
  71.2 0.9 copy-done.17
  72.1 0.9 copy-done.19
  73.1 0.9 copy-done.21
  74.0 0.9 copy-done.23
  75.0 3.3 %partial.1 = (f32[256,512]{1,0:T(8,128)S(1)}, bf16[256,512]{1,0:T(8,128)(2,1)}, bf16[256,512]{1,0:T(8,128)(2,1)}, bf16[256,512]{1,0:T(8,128)(2,1)}) custom-call(bf16[256,1024]{1,0:T(8,128)(2,1)S(1)} %copy-done.11, bf16[256,1024]{1,0:T(8,128)(2,1)S(1)} %copy-done.13, bf16[256,1024]{1,0:T(8,128)(2,1)S(1)} %copy-done.15, ...), custom_call_target="tpu_custom_call" | custom-call | flops 1073741824 | bytes 5242880 | tf_op jit(solution)/shard_map/partial/pallas_call | solution.py:112
  79.0 3.3 %collective-permute-start.6 = (bf16[256,512]{1,0:T(8,128)(2,1)}, bf16[256,512]{1,0:T(8,128)(2,1)}, u32[]{:S(2)}, u32[]{:S(2)}) collective-permute-start(bf16[256,512]{1,0:T(8,128)(2,1)} %get-tuple-element.26), channel_id=1, source_target_pairs={{0,1},{1,2},{2,3},{3,0},{4,5},{5,6},{6,7},{7,4},{8,9},{9,10},{10,1... | collective-permute-start | bytes 786440 | tf_op jit(solution)/shard_map/ppermute | solution.py:226
  82.4 3.8 %collective-permute-start.7 = (bf16[256,512]{1,0:T(8,128)(2,1)}, bf16[256,512]{1,0:T(8,128)(2,1)}, u32[]{:S(2)}, u32[]{:S(2)}) collective-permute-start(bf16[256,512]{1,0:T(8,128)(2,1)} %get-tuple-element.27), channel_id=1, source_target_pairs={{0,2},{1,3},{2,0},{3,1},{4,6},{5,7},{6,4},{7,5},{8,10},{9,11},{10,... | collective-permute-start | bytes 786440 | tf_op jit(solution)/shard_map/ppermute | solution.py:226
  86.2 3.9 %collective-permute-start.8 = (bf16[256,512]{1,0:T(8,128)(2,1)}, bf16[256,512]{1,0:T(8,128)(2,1)}, u32[]{:S(2)}, u32[]{:S(2)}) collective-permute-start(bf16[256,512]{1,0:T(8,128)(2,1)} %get-tuple-element.28), channel_id=1, source_target_pairs={{0,3},{1,0},{2,1},{3,2},{4,7},{5,4},{6,5},{7,6},{8,11},{9,8},{10,9... | collective-permute-start | bytes 786440 | tf_op jit(solution)/shard_map/ppermute | solution.py:226
  90.2 1.3 %dynamic-slice_convert_fusion.anchor = f32[8,512]{1,0:T(8,128)} fusion(bf16[256,512]{1,0:T(8,128)(2,1)} %param.11, s32[]{:T(128)S(6)} %select_n.3), kind=kLoop, calls=%fused_computation.2 | loop fusion | flops 4096 | bytes 24580 | tf_op jit(solution)/shard_map/convert_element_type | solution.py:228
  95.2 12.2 %all-to-all-start.1 = ((bf16[32,8,512]{2,1,0:T(8,128)(2,1)}), bf16[32,8,512]{2,1,0:T(8,128)(2,1)S(1)}, u32[]{:S(2)}, u32[]{:S(2)}) async-start(bf16[32,8,512]{2,1,0:T(8,128)(2,1)} %bitcast.9), calls=%async_computation.1 | async-start | bytes 524288 | tf_op jit(solution)/shard_map/all_to_all | solution.py:212
  107.5 6.5 %finish.1 = bf16[256,4096]{1,0:T(8,128)(2,1)} custom-call(bf16[256,4096]{1,0:T(8,128)(2,1)S(1)} %copy-done.1, f32[1,4096]{1,0:T(1,128)S(1)} %bitcast.11, f32[256,128]{1,0:T(8,128)S(1)} %get-tuple-element.29.inv_in, bf16[256,1024]{1,0:T(8,128)(2,1)S(1)} %get-tuple-element.30.refs_0_, bf16[256,1024]{1,0:T(8,128)(2,1)S(1)} %collective-permute-done.12.refs_1_, ...), custom_call_target="tpu_custom_call" | custom-call | flops 6291456 | bytes 6291456 | tf_op jit(solution)/shard_map/finish/pallas_call | solution.py:142
  114.0 2.0 %fusion = bf16[1,256,512]{2,1,0:T(8,128)(2,1)} fusion(bf16[256,512]{1,0:T(8,128)(2,1)} %collective-permute-done.8, bf16[256,512]{1,0:T(8,128)(2,1)} %collective-permute-done.7, f32[256,512]{1,0:T(8,128)S(1)} %copy-done.3, bf16[256,512]{1,0:T(8,128)(2,1)} %collective-permute-done.6), kind=kLoop, calls=%fused_computation.1 | loop fusion | flops 917504 | bytes 1572864 | tf_op jit(solution)/shard_map/broadcast_in_dim | solution.py:233
  116.0 8.0 %all-to-all-done.1 = bf16[32,8,512]{2,1,0:T(8,128)(2,1)S(1)} async-done(((bf16[32,8,512]{2,1,0:T(8,128)(2,1)}), bf16[32,8,512]{2,1,0:T(8,128)(2,1)S(1)}, u32[]{:S(2)}, u32[]{:S(2)}) %all-to-all-start.1) | async-done | bytes 262176 | tf_op jit(solution)/shard_map/all_to_all | solution.py:212
  (58 shorter events, 8.4 us)
Async XLA Ops:
  0.6 18.7 %collective-permute-start.3 = (bf16[256,512]{1,0:T(8,128)(2,1)}, bf16[256,512]{1,0:T(8,128)(2,1)S(1)}, u32[]{:S(2)}, u32[]{:S(2)}) collective-permute-start(bf16[256,512]{1,0:T(8,128)(2,1)} %refs_0_.1), channel_id=1, source_target_pairs={{0,4},{1,5},{2,6},{3,7},{4,8},{5,9},{6,10},{7,11},{8,12},{9,13},{1... | collective-permute-start | bytes 786440 | tf_op jit(solution)/shard_map/ppermute | solution.py:216
  4.0 25.2 %collective-permute-start.4 = (bf16[256,512]{1,0:T(8,128)(2,1)}, bf16[256,512]{1,0:T(8,128)(2,1)S(1)}, u32[]{:S(2)}, u32[]{:S(2)}) collective-permute-start(bf16[256,512]{1,0:T(8,128)(2,1)} %refs_0_.1), channel_id=1, source_target_pairs={{0,8},{1,9},{2,10},{3,11},{4,12},{5,13},{6,14},{7,15},{8,0},{9,1},... | collective-permute-start | bytes 786440 | tf_op jit(solution)/shard_map/ppermute | solution.py:216
  8.7 23.3 %collective-permute-start.5 = (bf16[256,512]{1,0:T(8,128)(2,1)}, bf16[256,512]{1,0:T(8,128)(2,1)S(1)}, u32[]{:S(2)}, u32[]{:S(2)}) collective-permute-start(bf16[256,512]{1,0:T(8,128)(2,1)} %refs_0_.1), channel_id=1, source_target_pairs={{0,12},{1,13},{2,14},{3,15},{4,0},{5,1},{6,2},{7,3},{8,4},{9,5},{1... | collective-permute-start | bytes 786440 | tf_op jit(solution)/shard_map/ppermute | solution.py:216
  12.0 23.9 %collective-permute-start.10 = (bf16[256,512]{1,0:T(8,128)(2,1)}, bf16[256,512]{1,0:T(8,128)(2,1)S(1)}, u32[]{:S(2)}, u32[]{:S(2)}) collective-permute-start(bf16[256,512]{1,0:T(8,128)(2,1)} %bitcast.2.refs_4_), channel_id=1, source_target_pairs={{0,2},{1,3},{2,0},{3,1},{4,6},{5,7},{6,4},{7,5},{8,10},{9,11},{10,... | collective-permute-start | bytes 786440 | tf_op jit(solution)/shard_map/ppermute | solution.py:215
  16.5 24.0 %collective-permute-start.11 = (bf16[256,512]{1,0:T(8,128)(2,1)}, bf16[256,512]{1,0:T(8,128)(2,1)S(1)}, u32[]{:S(2)}, u32[]{:S(2)}) collective-permute-start(bf16[256,512]{1,0:T(8,128)(2,1)} %bitcast.2.refs_4_), channel_id=1, source_target_pairs={{0,3},{1,0},{2,1},{3,2},{4,7},{5,4},{6,5},{7,6},{8,11},{9,8},{10,9... | collective-permute-start | bytes 786440 | tf_op jit(solution)/shard_map/ppermute | solution.py:215
  19.3 24.5 %copy-start.18 = (bf16[256,512]{1,0:T(8,128)(2,1)}, bf16[256,512]{1,0:T(8,128)(2,1)S(1)}, u32[]{:S(2)}) copy-start(bf16[256,512]{1,0:T(8,128)(2,1)S(1)} %collective-permute-done.3.refs_5_.refs_3_) | copy-start | bytes 786436
  19.3 21.2 %collective-permute-start.9 = (bf16[256,512]{1,0:T(8,128)(2,1)}, bf16[256,512]{1,0:T(8,128)(2,1)S(1)}, u32[]{:S(2)}, u32[]{:S(2)}) collective-permute-start(bf16[256,512]{1,0:T(8,128)(2,1)} %bitcast.2.refs_4_), channel_id=1, source_target_pairs={{0,1},{1,2},{2,3},{3,0},{4,5},{5,6},{6,7},{7,4},{8,9},{9,10},{10,1... | collective-permute-start | bytes 786440 | tf_op jit(solution)/shard_map/ppermute | solution.py:215
  22.7 1.6 %copy-start = (bf16[256,4096]{1,0:T(8,128)(2,1)S(1)}, bf16[256,4096]{1,0:T(8,128)(2,1)}, u32[]{:S(2)}) copy-start(bf16[256,4096]{1,0:T(8,128)(2,1)} %tokens.3) | copy-start | bytes 6291460
  25.0 15.5 %copy-start.16 = (bf16[256,512]{1,0:T(8,128)(2,1)S(1)}, bf16[256,512]{1,0:T(8,128)(2,1)}, u32[]{:S(2)}) copy-start(bf16[256,512]{1,0:T(8,128)(2,1)} %refs_0_.1) | copy-start | bytes 786436
  29.2 14.6 %copy-start.20 = (bf16[256,512]{1,0:T(8,128)(2,1)}, bf16[256,512]{1,0:T(8,128)(2,1)S(1)}, u32[]{:S(2)}) copy-start(bf16[256,512]{1,0:T(8,128)(2,1)S(1)} %collective-permute-done.4.refs_6_.refs_2_) | copy-start | bytes 786436
  29.2 33.8 %collective-permute-start = (bf16[256,1024]{1,0:T(8,128)(2,1)}, bf16[256,1024]{1,0:T(8,128)(2,1)S(1)}, u32[]{:S(2)}, u32[]{:S(2)}) collective-permute-start(bf16[256,1024]{1,0:T(8,128)(2,1)} %get-tuple-element.22), channel_id=1, source_target_pairs={{0,4},{1,5},{2,6},{3,7},{4,8},{5,9},{6,10},{7,11},{8,12},{9,13},{1... | collective-permute-start | bytes 1572872 | tf_op jit(solution)/shard_map/ppermute | solution.py:218
  32.0 13.8 %copy-start.22 = (bf16[256,512]{1,0:T(8,128)(2,1)}, bf16[256,512]{1,0:T(8,128)(2,1)S(1)}, u32[]{:S(2)}) copy-start(bf16[256,512]{1,0:T(8,128)(2,1)S(1)} %collective-permute-done.5.refs_7_.refs_1_) | copy-start | bytes 786436
  32.0 35.2 %collective-permute-start.1 = (bf16[256,1024]{1,0:T(8,128)(2,1)S(1)}, bf16[256,1024]{1,0:T(8,128)(2,1)S(1)}, u32[]{:S(2)}, u32[]{:S(2)}) collective-permute-start(bf16[256,1024]{1,0:T(8,128)(2,1)S(1)} %get-tuple-element.23), channel_id=1, source_target_pairs={{0,8},{1,9},{2,10},{3,11},{4,12},{5,13},{6,14},{7,15},{8,0},{9,1},... | collective-permute-start | bytes 1572872 | tf_op jit(solution)/shard_map/ppermute | solution.py:218
  36.0 32.1 %collective-permute-start.2 = (bf16[256,1024]{1,0:T(8,128)(2,1)S(1)}, bf16[256,1024]{1,0:T(8,128)(2,1)}, u32[]{:S(2)}, u32[]{:S(2)}) collective-permute-start(bf16[256,1024]{1,0:T(8,128)(2,1)S(1)} %get-tuple-element.24), channel_id=1, source_target_pairs={{0,12},{1,13},{2,14},{3,15},{4,0},{5,1},{6,2},{7,3},{8,4},{9,5},{1... | collective-permute-start | bytes 1572872 | tf_op jit(solution)/shard_map/ppermute | solution.py:218
  43.8 42.4 %collective-permute-start.12 = (bf16[256,1024]{1,0:T(8,128)(2,1)}, bf16[256,1024]{1,0:T(8,128)(2,1)S(1)}, u32[]{:S(2)}, u32[]{:S(2)}) collective-permute-start(bf16[256,1024]{1,0:T(8,128)(2,1)} %get-tuple-element.31), channel_id=1, source_target_pairs={{0,4},{1,5},{2,6},{3,7},{4,8},{5,9},{6,10},{7,11},{8,12},{9,13},{1... | collective-permute-start | bytes 1572872 | tf_op jit(solution)/shard_map/ppermute | solution.py:221
  45.8 45.7 %all-to-all-start = ((bf16[32,8,512]{2,1,0:T(8,128)(2,1)}), bf16[32,8,512]{2,1,0:T(8,128)(2,1)S(1)}, u32[]{:S(2)}, u32[]{:S(2)}) async-start(bf16[32,8,512]{2,1,0:T(8,128)(2,1)} %bitcast.3), calls=%async_computation | async-start | bytes 524288 | tf_op jit(solution)/shard_map/all_to_all | solution.py:212
  59.9 47.5 %collective-permute-start.13 = (bf16[256,1024]{1,0:T(8,128)(2,1)}, bf16[256,1024]{1,0:T(8,128)(2,1)}, u32[]{:S(2)}, u32[]{:S(2)}) collective-permute-start(bf16[256,1024]{1,0:T(8,128)(2,1)} %get-tuple-element.32), channel_id=1, source_target_pairs={{0,8},{1,9},{2,10},{3,11},{4,12},{5,13},{6,14},{7,15},{8,0},{9,1},... | collective-permute-start | bytes 1572872 | tf_op jit(solution)/shard_map/ppermute | solution.py:221
  63.8 43.6 %collective-permute-start.14 = (bf16[256,1024]{1,0:T(8,128)(2,1)}, bf16[256,1024]{1,0:T(8,128)(2,1)}, u32[]{:S(2)}, u32[]{:S(2)}) collective-permute-start(bf16[256,1024]{1,0:T(8,128)(2,1)} %get-tuple-element.33), channel_id=1, source_target_pairs={{0,12},{1,13},{2,14},{3,15},{4,0},{5,1},{6,2},{7,3},{8,4},{9,5},{1... | collective-permute-start | bytes 1572872 | tf_op jit(solution)/shard_map/ppermute | solution.py:221
  68.1 1.0 copy-start.11
  69.1 1.0 copy-start.13
  70.1 1.0 copy-start.15
  71.2 0.9 copy-start.17
  72.1 0.9 copy-start.19
  73.1 0.9 copy-start.21
  74.0 0.9 copy-start.23
  75.0 32.5 %copy-start.1 = (bf16[256,4096]{1,0:T(8,128)(2,1)S(1)}, bf16[256,4096]{1,0:T(8,128)(2,1)}, u32[]{:S(2)}) copy-start(bf16[256,4096]{1,0:T(8,128)(2,1)} %tokens.3) | copy-start | bytes 6291460
  75.0 32.5 %copy-start.6 = (f32[4096]{0:T(1024)S(1)}, f32[4096]{0:T(1024)}, u32[]{:S(2)}) copy-start(f32[4096]{0:T(1024)} %param.9) | copy-start | bytes 49156
  79.0 34.9 %collective-permute-start.6 = (bf16[256,512]{1,0:T(8,128)(2,1)}, bf16[256,512]{1,0:T(8,128)(2,1)}, u32[]{:S(2)}, u32[]{:S(2)}) collective-permute-start(bf16[256,512]{1,0:T(8,128)(2,1)} %get-tuple-element.26), channel_id=1, source_target_pairs={{0,1},{1,2},{2,3},{3,0},{4,5},{5,6},{6,7},{7,4},{8,9},{9,10},{10,1... | collective-permute-start | bytes 786440 | tf_op jit(solution)/shard_map/ppermute | solution.py:226
  82.4 31.6 %collective-permute-start.7 = (bf16[256,512]{1,0:T(8,128)(2,1)}, bf16[256,512]{1,0:T(8,128)(2,1)}, u32[]{:S(2)}, u32[]{:S(2)}) collective-permute-start(bf16[256,512]{1,0:T(8,128)(2,1)} %get-tuple-element.27), channel_id=1, source_target_pairs={{0,2},{1,3},{2,0},{3,1},{4,6},{5,7},{6,4},{7,5},{8,10},{9,11},{10,... | collective-permute-start | bytes 786440 | tf_op jit(solution)/shard_map/ppermute | solution.py:226
  86.2 27.7 %collective-permute-start.8 = (bf16[256,512]{1,0:T(8,128)(2,1)}, bf16[256,512]{1,0:T(8,128)(2,1)}, u32[]{:S(2)}, u32[]{:S(2)}) collective-permute-start(bf16[256,512]{1,0:T(8,128)(2,1)} %get-tuple-element.28), channel_id=1, source_target_pairs={{0,3},{1,0},{2,1},{3,2},{4,7},{5,4},{6,5},{7,6},{8,11},{9,8},{10,9... | collective-permute-start | bytes 786440 | tf_op jit(solution)/shard_map/ppermute | solution.py:226
  95.2 28.7 %all-to-all-start.1 = ((bf16[32,8,512]{2,1,0:T(8,128)(2,1)}), bf16[32,8,512]{2,1,0:T(8,128)(2,1)S(1)}, u32[]{:S(2)}, u32[]{:S(2)}) async-start(bf16[32,8,512]{2,1,0:T(8,128)(2,1)} %bitcast.9), calls=%async_computation.1 | async-start | bytes 524288 | tf_op jit(solution)/shard_map/all_to_all | solution.py:212
  107.5 6.5 %copy-start.3 = (f32[256,512]{1,0:T(8,128)S(1)}, f32[256,512]{1,0:T(8,128)}, u32[]{:S(2)}) copy-start(f32[256,512]{1,0:T(8,128)} %copy-done.2) | copy-start | bytes 1572868
  (9 other events, 6.8 us)

commit v2 on v1

v2 whole, which is shorter than its diff:
```python
import functools

import jax
import jax.numpy as jnp
from jax import lax
from jax.experimental import pallas as pl
from jax.experimental.pallas import tpu as pltpu
from jax.sharding import PartitionSpec as P

scale_eps = 1e-06
code_range = 448.0
norm_eps = 1e-05
outer_mu = 0.9
outer_rate = 0.7

SIDE = 4
ROWS = 128
F32 = jnp.float32
BF16 = jnp.bfloat16
LARGE = pltpu.CompilerParams(vmem_limit_bytes=60 * 1024 * 1024)
PARAMS = pltpu.CompilerParams(vmem_limit_bytes=30 * 1024 * 1024)
COST = pl.CostEstimate(flops=1, bytes_accessed=1, transcendentals=0)


def coords():
    index = lax.axis_index("fsdp")
    return index // SIDE, index % SIDE


def along_x(k):
    return [(x * SIDE + y, (x + k) % SIDE * SIDE + y) for x in range(SIDE) for y in range(SIDE)]


def along_y(k):
    return [(x * SIDE + y, x * SIDE + (y + k) % SIDE) for x in range(SIDE) for y in range(SIDE)]


def columns(step, width):
    return pl.ds(pl.multiple_of(step % SIDE * width, width), width)


def norm_kernel(tokens, cotangent, gain, inv_out, own_out, *packs):
    x, _ = coords()
    width = own_out.shape[1]
    full = tokens[...].astype(F32)
    inv = lax.rsqrt(jnp.mean(full * full, axis=-1, keepdims=True) + norm_eps)
    inv_out[...] = jnp.broadcast_to(inv, inv_out.shape)
    for k, out in enumerate((own_out,) + packs):
        cols = columns(x + k, width)
        out[:, :width] = (tokens[:, cols].astype(F32) * inv * gain[:, cols]).astype(BF16)
    for pack in packs:
        pack[:, width:] = cotangent[...]


def norm(tokens, cotangent, gain):
    count, width = tokens.shape
    part, keys = width // SIDE, cotangent.shape[1]

    def rows_of(columns):
        return pl.BlockSpec((ROWS, columns), lambda i: (i, 0))

    return pl.pallas_call(
        norm_kernel,
        grid=(count // ROWS,),
        in_specs=[rows_of(width), rows_of(keys), pl.BlockSpec((1, width), lambda i: (0, 0))],
        out_specs=[rows_of(128), rows_of(part)] + [rows_of(part + keys)] * (SIDE - 1),
        out_shape=[jax.ShapeDtypeStruct((count, 128), F32), jax.ShapeDtypeStruct((count, part), BF16)]
        + [jax.ShapeDtypeStruct((count, part + keys), BF16)] * (SIDE - 1),
        compiler_params=LARGE,
        cost_estimate=COST,
        name="norm",
    )(tokens, cotangent, gain)


def keys_of(source, width):
    place = source.shape[1] // width - 1
    return pl.BlockSpec((source.shape[0], width), lambda i: (0, place))


def back_kernel(number, *refs):
    cots, weight, outs = refs[:number], refs[number], refs[number + 1 :]
    for cot, out in zip(cots, outs, strict=True):
        out[...] = lax.dot_general(
            cot[...], weight[...], (((1,), (1,)), ((), ())), preferred_element_type=F32
        ).astype(BF16)


def back(sources, weight):
    count = sources[0].shape[0]
    rows, width = weight.shape
    number, block = len(sources), rows // 2
    return pl.pallas_call(
        functools.partial(back_kernel, number),
        grid=(rows // block,),
        in_specs=[keys_of(source, width) for source in sources]
        + [pl.BlockSpec((block, width), lambda i: (i, 0))],
        out_specs=[pl.BlockSpec((count, block), lambda i: (0, i))] * number,
        out_shape=[jax.ShapeDtypeStruct((count, rows), BF16)] * number,
        compiler_params=PARAMS,
        cost_estimate=COST,
        name="back",
    )(*sources, weight)


def normed_of(source, rows):
    return pl.BlockSpec((source.shape[0], rows), lambda j: (0, j))


def partial_kernel(number, *refs):
    normed, cots, out = refs[:number], refs[number : 2 * number], refs[-1]
    total = jnp.zeros(out.shape, F32)
    for block, cot in zip(normed, cots, strict=True):
        total = total + lax.dot_general(
            block[...], cot[...], (((0,), (0,)), ((), ())), preferred_element_type=F32
        )
    out[...] = total.astype(BF16)


def partial(own, cotangent, packs):
    width = cotangent.shape[1]
    rows = own.shape[1] // 2
    return pl.pallas_call(
        functools.partial(partial_kernel, len(packs) + 1),
        grid=(2,),
        in_specs=[normed_of(source, rows) for source in (own, *packs)]
        + [keys_of(source, width) for source in (cotangent, *packs)],
        out_specs=pl.BlockSpec((rows, width), lambda j: (j, 0)),
        out_shape=jax.ShapeDtypeStruct((own.shape[1], width), BF16),
        compiler_params=PARAMS,
        cost_estimate=COST,
        name="partial",
    )(own, *packs, cotangent, *packs)


def finish_kernel(tokens, gain, inv_in, *refs):
    pieces, out = refs[:SIDE], refs[SIDE]
    x, _ = coords()
    width = pieces[0].shape[1]
    inv = inv_in[:, :1]
    total = jnp.zeros(inv.shape, F32)
    for k, piece in zip((2, 1, 3, 0), pieces, strict=True):
        cols = columns(x - k + SIDE, width)
        scaled = piece[...].astype(F32) * gain[:, cols]
        total = total + jnp.sum(tokens[:, cols].astype(F32) * scaled, axis=-1, keepdims=True)
    factor = inv * inv * inv * (total / (SIDE * width))
    for k, piece in zip((2, 1, 3, 0), pieces, strict=True):
        cols = columns(x - k + SIDE, width)
        scaled = piece[...].astype(F32) * gain[:, cols]
        out[:, cols] = (inv * scaled - tokens[:, cols].astype(F32) * factor).astype(BF16)


def finish(tokens, gain, inv, pieces):
    count, width = tokens.shape
    part = width // SIDE
    return pl.pallas_call(
        finish_kernel,
        grid=(count // ROWS,),
        in_specs=[
            pl.BlockSpec((ROWS, width), lambda i: (i, 0)),
            pl.BlockSpec((1, width), lambda i: (0, 0)),
            pl.BlockSpec((ROWS, 128), lambda i: (i, 0)),
        ]
        + [pl.BlockSpec((ROWS, part), lambda i: (i, 0))] * SIDE,
        out_specs=pl.BlockSpec((ROWS, width), lambda i: (i, 0)),
        out_shape=jax.ShapeDtypeStruct((count, width), BF16),
        compiler_params=LARGE,
        cost_estimate=COST,
        name="finish",
    )(tokens, gain, inv, *pieces)


def requantized(values):
    parts = []
    for start in range(0, values.shape[-1], 128):
        block = values[..., start : start + 128]
        peak = jnp.max(jnp.abs(block), axis=-1, keepdims=True)
        scale = ((peak + scale_eps) / code_range).astype(BF16).astype(F32)
        parts.append((block / scale).astype(BF16).astype(F32) * scale)
    return jnp.concatenate(parts, axis=-1)


def outer_kernel(local, anchor, master, moment, master_out, moment_out, synced_out):
    slab = master.shape[0]
    replicas = local.shape[0] // slab
    pair = anchor[...].astype(F32)
    start = jnp.where(lax.axis_index("rep") % 2 == 0, pair[:slab], pair[slab:])
    total = jnp.zeros(start.shape, F32)
    held = local[...].astype(F32)
    for r in range(replicas):
        total = total + requantized(start - held[r * slab : (r + 1) * slab])
    pseudo = total / replicas
    new_moment = outer_mu * moment[...] + pseudo
    step = outer_rate * (pseudo + outer_mu * new_moment)
    moment_out[...] = new_moment
    master_out[...] = master[...] - step
    synced = start - requantized(step)
    synced_out[...] = jnp.concatenate([synced] * replicas, axis=0).astype(BF16)


def outer(local, anchor, master, moment):
    slab, width = master.shape
    own = pl.BlockSpec((slab, width), lambda i: (0, 0))
    whole = pl.BlockSpec(local.shape, lambda i: (0, 0))
    return pl.pallas_call(
        outer_kernel,
        grid=(1,),
        in_specs=[whole, pl.BlockSpec((2 * slab, width), lambda i: (lax.axis_index("rep") // 2, 0)), own, own],
        out_specs=[own, own, whole],
        out_shape=[
            jax.ShapeDtypeStruct((slab, width), F32),
            jax.ShapeDtypeStruct((slab, width), F32),
            jax.ShapeDtypeStruct(local.shape, BF16),
        ],
        compiler_params=PARAMS,
        cost_estimate=COST,
        name="outer",
    )(local, anchor, master, moment)


def local(tokens, cotangent, norm_gain, local_weight, anchor_weight, outer_master, outer_moment):
    key_width = cotangent.shape[1]
    weight = local_weight[0]
    own_rows = weight.shape[0]
    replicas = lax.axis_size("rep")
    slab = own_rows // replicas
    gain = norm_gain[None]

    def exchange(block):
        split = block.reshape(replicas, slab, key_width)
        return lax.all_to_all(split, "rep", split_axis=0, concat_axis=0, tiled=True).reshape(own_rows, key_width)

    line = [[x * SIDE + y for y in range(SIDE)] for x in range(SIDE)]
    weights = lax.all_gather(weight, "fsdp", axis=0, tiled=True, axis_index_groups=line)
    inv, own, *packs = norm(tokens, cotangent, gain)
    second = lax.ppermute(packs[1], "fsdp", along_x(2))
    packs = [lax.ppermute(packs[0], "fsdp", along_x(1)), second, lax.ppermute(packs[2], "fsdp", along_x(3))]
    gathered = exchange(weight)
    new_master, new_moment, synced = outer(gathered, anchor_weight, outer_master, outer_moment)

    own, _ = lax.optimization_barrier((own, synced))
    part = partial(own, cotangent, [packs[1], packs[0], packs[2]])
    grad_weight = lax.psum_scatter(part, "fsdp", scatter_dimension=0, tiled=True, axis_index_groups=line)

    weights, _ = lax.optimization_barrier((weights, part))
    across, ahead, behind, kept = back([packs[1], packs[2], packs[0], cotangent], weights)
    across = lax.ppermute(across, "fsdp", along_x(2))
    pieces = [across, lax.ppermute(ahead, "fsdp", along_x(1)), lax.ppermute(behind, "fsdp", along_x(3)), kept]

    synced, _ = lax.optimization_barrier((synced, kept))
    synced_weight = exchange(synced)
    grad_tokens = finish(tokens, gain, inv, pieces)
    synced_weight, grad_tokens = lax.optimization_barrier((synced_weight, grad_tokens))
    return (grad_weight[None], grad_tokens, synced_weight, new_master, new_moment)


def solution(mesh):
    in_specs = (
        P(("rep", "fsdp"), None),
        P(("rep", "fsdp"), None),
        P(),
        P("rep", "fsdp", None),
        P("fsdp", None),
        P(("fsdp", "rep"), None),
        P(("fsdp", "rep"), None),
    )
    out_specs = (
        P("rep", "fsdp", None),
        P(("rep", "fsdp"), None),
        P("fsdp", None),
        P(("fsdp", "rep"), None),
        P(("fsdp", "rep"), None),
    )
    return jax.shard_map(local, mesh=mesh, in_specs=in_specs, out_specs=out_specs, check_vma=False)
```

time: 126 us -> 115 us (0.913)
  starting transfers between devices: 79.1 us -> 29 us
  blocking collectives: 0 us -> 36.7 us
  between operations: 0.97 us -> 14.2 us
  local copies, waits for them, and re-layouts: 16 us -> 4.76 us
  waiting for transfers between devices: 8.02 us -> 15.2 us
  other arithmetic: 3.26 us -> 0 us
  Pallas kernels: 17.3 us -> 14.2 us
    all_to_all x0 -> x1, blocking collectives: none -> 36.7 us  [exchange(): lax.all_to_all(split, 'rep', split_axis=0, concat_axis=0, tiled=True)]
    ppermute x15 -> x6, starting transfers between devices: 52.8 us -> 20.9 us  [the longest x1 4.92 us: local(): second = lax.ppermute(packs[1], 'fsdp', along_x(2))]
    all_to_all x2 -> x1, starting transfers between devices: 26.3 us -> 8.01 us  [exchange(): lax.all_to_all(split, 'rep', split_axis=0, concat_axis=0, tiled=True)]
    unnamed x49 -> x23, local copies, waits for them, and re-layouts: 16 us -> 4.76 us
    ppermute x15 -> x6, waiting for transfers between devices: 0.04 us -> 10.6 us  [the longest x1 9.11 us: local(): lax.ppermute(ahead, 'fsdp', along_x(1))]
    all_to_all x2 -> x1, waiting for transfers between devices: 7.98 us -> 3.9 us  [exchange(): lax.all_to_all(split, 'rep', split_axis=0, concat_axis=0, tiled=True)]
    broadcast_in_dim x1 -> x0, other arithmetic: 1.95 us -> none  [local(): grad_weight.astype(BF16)[None]]
    pallas_call x1, Pallas kernels: 6.51 us -> 4.7 us  [finish(): pl.pallas_call(finish_kernel, grid=(count // ROWS,), in_specs=[pl.BlockSp...]
  transfers between devices with their start and end apart: 17 -> 9, of which waited for: 1 -> 3; matrix products, arithmetic and copies ran while one was open for 3% -> 0% of each run, Pallas kernels for 14% -> 12%
where the time goes in v2:
time: 115 us; the launch traced here: 114 us
  blocking collectives  36.7 us (32%)
  starting transfers between devices  29 us (25%)
  waiting for transfers between devices  15.2 us (13%)
  Pallas kernels  14.2 us (12%)
  between operations  14.2 us (12%)
  local copies, waits for them, and re-layouts  4.76 us (4%)
    all_to_all x1, blocking collectives, exchange(): lax.all_to_all(split, 'rep', split_axis=0, concat_axis=0, tiled=True)  36.7 us
    ppermute x1, waiting for transfers between devices, local(): lax.ppermute(ahead, 'fsdp', along_x(1))  9.11 us
    all_to_all x1, starting transfers between devices, exchange(): lax.all_to_all(split, 'rep', split_axis=0, concat_axis=0, tiled=True)  8.01 us
    ppermute x1, starting transfers between devices, local(): second = lax.ppermute(packs[1], 'fsdp', along_x(2))  4.92 us
    unnamed x23, local copies, waits for them, and re-layouts  4.76 us
    pallas_call x1, Pallas kernels, finish(): pl.pallas_call(finish_kernel, grid=(count // ROWS,), in_specs=[pl.BlockSp...  4.7 us
    ppermute x1, starting transfers between devices, local(): lax.ppermute(packs[2], 'fsdp', along_x(3))  4.55 us
    ppermute x1, starting transfers between devices, local(): lax.ppermute(behind, 'fsdp', along_x(3))  4.29 us
  transfers between devices with their start and end apart: 9, of which 3 were waited for; matrix products, arithmetic and copies ran while one was open for 0% of the time, Pallas kernels for 12%

profile of v2, /device:TPU:8, one launch (start us, length us, event | category | flops | bytes accessed | tf_op | source)
XLA Modules:
  0.0 114.1 jit_solution(3242650557502654783)
XLA Ops:
  7.2 0.0 all-gather.3.cloned.1.call-start
  7.3 0.7 all-gather.3.cloned.1.call-update
  8.0 0.0 reduce-scatter.2.cloned.1.call-start
  8.0 3.7 %norm.1 = (f32[256,128]{1,0:T(8,128)}, bf16[256,1024]{1,0:T(8,128)(2,1)}, bf16[256,1536]{1,0:T(8,128)(2,1)}, bf16[256,1536]{1,0:T(8,128)(2,1)}, bf16[256,1536]{1,0:T(8,128)(2,1)}) custom-call(bf16[256,4096]{1,0:T(8,128)(2,1)} %tokens.3, bf16[256,512]{1,0:T(8,128)(2,1)} %refs_3_.1, f32[1,4096]{1,0:T(1,128)} %bitcast.11), custom_call_target="tpu_custom_call" | custom-call | flops 1 | bytes 1 | tf_op jit(solution)/shard_map/norm/pallas_call | solution.py:62
  11.7 4.9 %collective-permute-start = (bf16[256,1536]{1,0:T(8,128)(2,1)}, bf16[256,1536]{1,0:T(8,128)(2,1)S(1)}, u32[]{:S(2)}, u32[]{:S(2)}) collective-permute-start(bf16[256,1536]{1,0:T(8,128)(2,1)} %get-tuple-element.25), channel_id=1, source_target_pairs={{0,8},{1,9},{2,10},{3,11},{4,12},{5,13},{6,14},{7,15},{8,0},{9,1},... | collective-permute-start | bytes 2359304 | tf_op jit(solution)/shard_map/ppermute | solution.py:235
  16.6 2.5 %collective-permute-start.1 = (bf16[256,1536]{1,0:T(8,128)(2,1)}, bf16[256,1536]{1,0:T(8,128)(2,1)S(1)}, u32[]{:S(2)}, u32[]{:S(2)}) collective-permute-start(bf16[256,1536]{1,0:T(8,128)(2,1)} %get-tuple-element.26), channel_id=1, source_target_pairs={{0,4},{1,5},{2,6},{3,7},{4,8},{5,9},{6,10},{7,11},{8,12},{9,13},{1... | collective-permute-start | bytes 2359304 | tf_op jit(solution)/shard_map/ppermute | solution.py:236
  19.1 4.6 %collective-permute-start.2 = (bf16[256,1536]{1,0:T(8,128)(2,1)}, bf16[256,1536]{1,0:T(8,128)(2,1)S(1)}, u32[]{:S(2)}, u32[]{:S(2)}) collective-permute-start(bf16[256,1536]{1,0:T(8,128)(2,1)} %get-tuple-element.27), channel_id=1, source_target_pairs={{0,12},{1,13},{2,14},{3,15},{4,0},{5,1},{6,2},{7,3},{8,4},{9,5},{1... | collective-permute-start | bytes 2359304 | tf_op jit(solution)/shard_map/ppermute | solution.py:236
  23.7 0.0 copy-done.7
  23.7 36.7 %all_to_all.10 = bf16[32,8,512]{2,1,0:T(8,128)(2,1)S(1)} all-to-all(bf16[32,8,512]{2,1,0:T(8,128)(2,1)S(1)} %bitcast.9), channel_id=1, replica_groups=mesh['rep'=32,'fsdp'=16] {'rep'}, dimensions={0} | all-to-all | bytes 524288 | tf_op jit(solution)/shard_map/all_to_all | solution.py:230
  60.4 1.1 outer.1
  61.5 0.0 collective-permute-done.refs_1_.refs_5_.refs_0_
  61.5 0.0 collective-permute-done.1.refs_2_.refs_6_
  61.5 0.0 collective-permute-done.2.refs_3_.refs_7_.refs_1_
  61.5 1.0 copy-done.3
  62.6 2.5 %partial.1 = bf16[1024,512]{1,0:T(8,128)(2,1)} custom-call(bf16[256,1024]{1,0:T(8,128)(2,1)S(1)} %copy-done.3, bf16[256,1536]{1,0:T(8,128)(2,1)S(1)} %collective-permute-done.refs_1_.refs_5_.refs_0_, bf16[256,1536]{1,0:T(8,128)(2,1)S(1)} %collective-permute-done.1.refs_2_.refs_6_, bf16[256,1536]{1,0:T(8,128)(2,1)S(1)} %collective-permute-done.2.refs_3_.refs_7_.refs_1_, ...), custom_call_target="tpu_custom_call" | custom-call | flops 1 | bytes 1 | tf_op jit(solution)/shard_map/partial/pallas_call | solution.py:122
  65.1 0.0 reduce-scatter.2.cloned.1.call-update
  65.1 0.0 all-gather.3.cloned.1.call-done
  65.2 1.2 %copy-done.1 = bf16[1,1024,512]{2,1,0:T(8,128)(2,1)S(1)} copy-done((bf16[1,1024,512]{2,1,0:T(8,128)(2,1)S(1)}, bf16[1,1024,512]{2,1,0:T(8,128)(2,1)}, u32[]{:S(2)}) %copy-start.1) | copy-done | bytes 1048600
  66.4 2.1 %back.1 = (bf16[256,1024]{1,0:T(8,128)(2,1)}, bf16[256,1024]{1,0:T(8,128)(2,1)}, bf16[256,1024]{1,0:T(8,128)(2,1)S(1)}, bf16[256,1024]{1,0:T(8,128)(2,1)S(1)}) custom-call(bf16[256,1536]{1,0:T(8,128)(2,1)S(1)} %collective-permute-done.refs_1_.refs_5_.refs_0_, bf16[256,1536]{1,0:T(8,128)(2,1)S(1)} %collective-permute-done.2.refs_3_.refs_7_.refs_1_, ...), custom_call_target="tpu_custom_call" | custom-call | flops 1 | bytes 1 | tf_op jit(solution)/shard_map/back/pallas_call | solution.py:92
  68.5 0.8 copy-done.2
  69.3 1.9 %collective-permute-start.3 = (bf16[256,1024]{1,0:T(8,128)(2,1)}, bf16[256,1024]{1,0:T(8,128)(2,1)S(1)}, u32[]{:S(2)}, u32[]{:S(2)}) collective-permute-start(bf16[256,1024]{1,0:T(8,128)(2,1)} %get-tuple-element.32), channel_id=1, source_target_pairs={{0,8},{1,9},{2,10},{3,11},{4,12},{5,13},{6,14},{7,15},{8,0},{9,1},... | collective-permute-start | bytes 1572872 | tf_op jit(solution)/shard_map/ppermute | solution.py:246
  71.2 2.8 %collective-permute-start.4 = (bf16[256,1024]{1,0:T(8,128)(2,1)}, bf16[256,1024]{1,0:T(8,128)(2,1)S(1)}, u32[]{:S(2)}, u32[]{:S(2)}) collective-permute-start(bf16[256,1024]{1,0:T(8,128)(2,1)} %get-tuple-element.33), channel_id=1, source_target_pairs={{0,4},{1,5},{2,6},{3,7},{4,8},{5,9},{6,10},{7,11},{8,12},{9,13},{1... | collective-permute-start | bytes 1572872 | tf_op jit(solution)/shard_map/ppermute | solution.py:247
  74.0 4.3 %collective-permute-start.5 = (bf16[256,1024]{1,0:T(8,128)(2,1)S(1)}, bf16[256,1024]{1,0:T(8,128)(2,1)S(1)}, u32[]{:S(2)}, u32[]{:S(2)}) collective-permute-start(bf16[256,1024]{1,0:T(8,128)(2,1)S(1)} %get-tuple-element.34), channel_id=1, source_target_pairs={{0,12},{1,13},{2,14},{3,15},{4,0},{5,1},{6,2},{7,3},{8,4},{9,5},{1... | collective-permute-start | bytes 1572872 | tf_op jit(solution)/shard_map/ppermute | solution.py:247
  78.3 8.0 %all-to-all-start.1 = ((bf16[32,8,512]{2,1,0:T(8,128)(2,1)}), bf16[32,8,512]{2,1,0:T(8,128)(2,1)S(1)}, u32[]{:S(2)}, u32[]{:S(2)}) async-start(bf16[32,8,512]{2,1,0:T(8,128)(2,1)} %bitcast.5), calls=%async_computation.2 | async-start | bytes 524288 | tf_op jit(solution)/shard_map/all_to_all | solution.py:230
  86.3 1.5 %collective-permute-done.3.refs_0_ = bf16[256,1024]{1,0:T(8,128)(2,1)S(1)} collective-permute-done((bf16[256,1024]{1,0:T(8,128)(2,1)}, bf16[256,1024]{1,0:T(8,128)(2,1)S(1)}, u32[]{:S(2)}, u32[]{:S(2)}) %collective-permute-start.3) | collective-permute-done | bytes 524320 | tf_op jit(solution)/shard_map/ppermute | solution.py:246
  87.8 9.1 %collective-permute-done.4.refs_1_ = bf16[256,1024]{1,0:T(8,128)(2,1)S(1)} collective-permute-done((bf16[256,1024]{1,0:T(8,128)(2,1)}, bf16[256,1024]{1,0:T(8,128)(2,1)S(1)}, u32[]{:S(2)}, u32[]{:S(2)}) %collective-permute-start.4) | collective-permute-done | bytes 524320 | tf_op jit(solution)/shard_map/ppermute | solution.py:247
  96.9 0.0 collective-permute-done.5.refs_2_
  96.9 0.8 copy-done.9
  97.7 0.2 copy-done.10
  97.9 4.7 %finish.1 = bf16[256,4096]{1,0:T(8,128)(2,1)} custom-call(bf16[256,4096]{1,0:T(8,128)(2,1)} %tokens.3, f32[1,4096]{1,0:T(1,128)} %bitcast.12, f32[256,128]{1,0:T(8,128)} %get-tuple-element.31.inv_in, bf16[256,1024]{1,0:T(8,128)(2,1)} %copy-done.8, bf16[256,1024]{1,0:T(8,128)(2,1)} %copy-done.9, bf16[256,1024]{1,0:T(8,128)(2,1)} %copy-done.10, ...), custom_call_target="tpu_custom_call" | custom-call | flops 1 | bytes 1 | tf_op jit(solution)/shard_map/finish/pallas_call | solution.py:155
  102.6 3.9 %all-to-all-done.1 = bf16[32,8,512]{2,1,0:T(8,128)(2,1)S(1)} async-done(((bf16[32,8,512]{2,1,0:T(8,128)(2,1)}), bf16[32,8,512]{2,1,0:T(8,128)(2,1)S(1)}, u32[]{:S(2)}, u32[]{:S(2)}) %all-to-all-start.1) | async-done | bytes 262176 | tf_op jit(solution)/shard_map/all_to_all | solution.py:230
  106.5 0.7 copy.13
  (17 shorter events, 0.0 us)
Async XLA Ops:
  7.2 16.5 %copy-start.7 = (bf16[1,256,512]{2,1,0:T(8,128)(2,1)S(1)}, bf16[1,256,512]{2,1,0:T(8,128)(2,1)}, u32[]{:S(2)}) copy-start(bf16[1,256,512]{2,1,0:T(8,128)(2,1)} %param.10) | copy-start | bytes 786436
  7.2 54.3 %copy-start = (bf16[256,512]{1,0:T(8,128)(2,1)S(1)}, bf16[256,512]{1,0:T(8,128)(2,1)}, u32[]{:S(2)}) copy-start(bf16[256,512]{1,0:T(8,128)(2,1)} %refs_3_.1) | copy-start | bytes 786436
  7.2 53.2 %copy-start.4 = (bf16[256,512]{1,0:T(8,128)(2,1)S(1)}, bf16[256,512]{1,0:T(8,128)(2,1)}, u32[]{:S(2)}) copy-start(bf16[256,512]{1,0:T(8,128)(2,1)} %anchor.1) | copy-start | bytes 786436
  7.2 53.2 %copy-start.5 = (f32[8,512]{1,0:T(8,128)S(1)}, f32[8,512]{1,0:T(8,128)}, u32[]{:S(2)}) copy-start(f32[8,512]{1,0:T(8,128)} %master.1) | copy-start | bytes 49156
  7.2 53.2 %copy-start.6 = (f32[8,512]{1,0:T(8,128)S(1)}, f32[8,512]{1,0:T(8,128)}, u32[]{:S(2)}) copy-start(f32[8,512]{1,0:T(8,128)} %moment.1) | copy-start | bytes 49156
  7.2 57.9 %all-gather.3.cloned.1.call-start = ((), (), s32[]{:S(2)}) async-start(), calls=%async_computation.4 | async-start | bytes 1310720 | tf_op jit(solution)/shard_map/all_gather | solution.py:233
  8.0 98.6 %reduce-scatter.2.cloned.1.call-start = ((), (), s32[]{:S(2)}) async-start(), calls=%async_computation.3 | async-start | bytes 1310720 | tf_op jit(solution)/shard_map/reduce_scatter | solution.py:242
  11.7 49.8 %collective-permute-start = (bf16[256,1536]{1,0:T(8,128)(2,1)}, bf16[256,1536]{1,0:T(8,128)(2,1)S(1)}, u32[]{:S(2)}, u32[]{:S(2)}) collective-permute-start(bf16[256,1536]{1,0:T(8,128)(2,1)} %get-tuple-element.25), channel_id=1, source_target_pairs={{0,8},{1,9},{2,10},{3,11},{4,12},{5,13},{6,14},{7,15},{8,0},{9,1},... | collective-permute-start | bytes 2359304 | tf_op jit(solution)/shard_map/ppermute | solution.py:235
  16.6 44.9 %collective-permute-start.1 = (bf16[256,1536]{1,0:T(8,128)(2,1)}, bf16[256,1536]{1,0:T(8,128)(2,1)S(1)}, u32[]{:S(2)}, u32[]{:S(2)}) collective-permute-start(bf16[256,1536]{1,0:T(8,128)(2,1)} %get-tuple-element.26), channel_id=1, source_target_pairs={{0,4},{1,5},{2,6},{3,7},{4,8},{5,9},{6,10},{7,11},{8,12},{9,13},{1... | collective-permute-start | bytes 2359304 | tf_op jit(solution)/shard_map/ppermute | solution.py:236
  19.1 42.4 %collective-permute-start.2 = (bf16[256,1536]{1,0:T(8,128)(2,1)}, bf16[256,1536]{1,0:T(8,128)(2,1)S(1)}, u32[]{:S(2)}, u32[]{:S(2)}) collective-permute-start(bf16[256,1536]{1,0:T(8,128)(2,1)} %get-tuple-element.27), channel_id=1, source_target_pairs={{0,12},{1,13},{2,14},{3,15},{4,0},{5,1},{6,2},{7,3},{8,4},{9,5},{1... | collective-permute-start | bytes 2359304 | tf_op jit(solution)/shard_map/ppermute | solution.py:236
  61.5 1.0 copy-start.3
  65.2 1.2 %copy-start.1 = (bf16[1,1024,512]{2,1,0:T(8,128)(2,1)S(1)}, bf16[1,1024,512]{2,1,0:T(8,128)(2,1)}, u32[]{:S(2)}) copy-start(bf16[1,1024,512]{2,1,0:T(8,128)(2,1)} %all-gather.3.cloned.1.call-done) | copy-start | bytes 3145732
  68.5 0.8 copy-start.2
  69.3 18.5 %collective-permute-start.3 = (bf16[256,1024]{1,0:T(8,128)(2,1)}, bf16[256,1024]{1,0:T(8,128)(2,1)S(1)}, u32[]{:S(2)}, u32[]{:S(2)}) collective-permute-start(bf16[256,1024]{1,0:T(8,128)(2,1)} %get-tuple-element.32), channel_id=1, source_target_pairs={{0,8},{1,9},{2,10},{3,11},{4,12},{5,13},{6,14},{7,15},{8,0},{9,1},... | collective-permute-start | bytes 1572872 | tf_op jit(solution)/shard_map/ppermute | solution.py:246
  71.2 25.7 %collective-permute-start.4 = (bf16[256,1024]{1,0:T(8,128)(2,1)}, bf16[256,1024]{1,0:T(8,128)(2,1)S(1)}, u32[]{:S(2)}, u32[]{:S(2)}) collective-permute-start(bf16[256,1024]{1,0:T(8,128)(2,1)} %get-tuple-element.33), channel_id=1, source_target_pairs={{0,4},{1,5},{2,6},{3,7},{4,8},{5,9},{6,10},{7,11},{8,12},{9,13},{1... | collective-permute-start | bytes 1572872 | tf_op jit(solution)/shard_map/ppermute | solution.py:247
  74.0 22.9 %collective-permute-start.5 = (bf16[256,1024]{1,0:T(8,128)(2,1)S(1)}, bf16[256,1024]{1,0:T(8,128)(2,1)S(1)}, u32[]{:S(2)}, u32[]{:S(2)}) collective-permute-start(bf16[256,1024]{1,0:T(8,128)(2,1)S(1)} %get-tuple-element.34), channel_id=1, source_target_pairs={{0,12},{1,13},{2,14},{3,15},{4,0},{5,1},{6,2},{7,3},{8,4},{9,5},{1... | collective-permute-start | bytes 1572872 | tf_op jit(solution)/shard_map/ppermute | solution.py:247
  78.3 28.2 %all-to-all-start.1 = ((bf16[32,8,512]{2,1,0:T(8,128)(2,1)}), bf16[32,8,512]{2,1,0:T(8,128)(2,1)S(1)}, u32[]{:S(2)}, u32[]{:S(2)}) async-start(bf16[32,8,512]{2,1,0:T(8,128)(2,1)} %bitcast.5), calls=%async_computation.2 | async-start | bytes 524288 | tf_op jit(solution)/shard_map/all_to_all | solution.py:230
  87.8 9.1 %copy-start.8 = (bf16[256,1024]{1,0:T(8,128)(2,1)}, bf16[256,1024]{1,0:T(8,128)(2,1)S(1)}, u32[]{:S(2)}) copy-start(bf16[256,1024]{1,0:T(8,128)(2,1)S(1)} %collective-permute-done.3.refs_0_) | copy-start | bytes 1572868
  96.9 0.8 copy-start.9
  96.9 1.0 copy-start.10
Sparse Core Ops, SparseCore 0:
  10.2 43.1 all-gather.2
  65.2 30.6 reduce-scatter.1

commit v3 on v2

--- a/solution.py
+++ b/solution.py
@@ -20,6 +20,8 @@
 LARGE = pltpu.CompilerParams(vmem_limit_bytes=60 * 1024 * 1024)
 PARAMS = pltpu.CompilerParams(vmem_limit_bytes=30 * 1024 * 1024)
 COST = pl.CostEstimate(flops=1, bytes_accessed=1, transcendentals=0)
+MIDDLE = pl.CostEstimate(flops=2 << 30, bytes_accessed=1, transcendentals=0)
+LONG = pl.CostEstimate(flops=1 << 35, bytes_accessed=1 << 28, transcendentals=0)
 
 
 def coords():
@@ -212,9 +214,23 @@
             jax.ShapeDtypeStruct(local.shape, BF16),
         ],
         compiler_params=PARAMS,
-        cost_estimate=COST,
+        cost_estimate=MIDDLE,
         name="outer",
     )(local, anchor, master, moment)
+
+
+def place_kernel(block, out):
+    out[...] = block[...]
+
+
+def place(block):
+    return pl.pallas_call(
+        place_kernel,
+        out_shape=jax.ShapeDtypeStruct(block.shape, block.dtype),
+        compiler_params=PARAMS,
+        cost_estimate=LONG,
+        name="place",
+    )(block)
 
 
 def local(tokens, cotangent, norm_gain, local_weight, anchor_weight, outer_master, outer_moment):
@@ -235,21 +251,19 @@
     second = lax.ppermute(packs[1], "fsdp", along_x(2))
     packs = [lax.ppermute(packs[0], "fsdp", along_x(1)), second, lax.ppermute(packs[2], "fsdp", along_x(3))]
     gathered = exchange(weight)
+    gathered, packs[1] = lax.optimization_barrier((gathered, packs[1]))
     new_master, new_moment, synced = outer(gathered, anchor_weight, outer_master, outer_moment)
+    synced_weight = place(exchange(synced))
 
     own, _ = lax.optimization_barrier((own, synced))
     part = partial(own, cotangent, [packs[1], packs[0], packs[2]])
     grad_weight = lax.psum_scatter(part, "fsdp", scatter_dimension=0, tiled=True, axis_index_groups=line)
-
     weights, _ = lax.optimization_barrier((weights, part))
     across, ahead, behind, kept = back([packs[1], packs[2], packs[0], cotangent], weights)
     across = lax.ppermute(across, "fsdp", along_x(2))
     pieces = [across, lax.ppermute(ahead, "fsdp", along_x(1)), lax.ppermute(behind, "fsdp", along_x(3)), kept]
-
-    synced, _ = lax.optimization_barrier((synced, kept))
-    synced_weight = exchange(synced)
+    inv, synced_weight = lax.optimization_barrier((inv, synced_weight))
     grad_tokens = finish(tokens, gain, inv, pieces)
-    synced_weight, grad_tokens = lax.optimization_barrier((synced_weight, grad_tokens))
     return (grad_weight[None], grad_tokens, synced_weight, new_master, new_moment)
 
 

time: 115 us -> 110 us (0.957)
  the two profiles are of different devices: /device:TPU:8 before, /device:TPU:41 now
where the time goes in v3:
time: 110 us; the launch traced here: 109 us
  starting transfers between devices  46.1 us (42%)
  waiting for transfers between devices  30 us (27%)
  Pallas kernels  14.4 us (13%)
  between operations  14.2 us (13%)
  local copies, waits for them, and re-layouts  4.66 us (4%)
    all_to_all x2, starting transfers between devices, exchange(): lax.all_to_all(split, 'rep', split_axis=0, concat_axis=0, tiled=True)  26.2 us
    ppermute x1, waiting for transfers between devices, local(): lax.ppermute(ahead, 'fsdp', along_x(1))  11.9 us
    all_to_all x2, waiting for transfers between devices, exchange(): lax.all_to_all(split, 'rep', split_axis=0, concat_axis=0, tiled=True)  9.93 us
    ppermute x1, waiting for transfers between devices, local(): across = lax.ppermute(across, 'fsdp', along_x(2))  7.39 us
    pallas_call x1, Pallas kernels, finish(): pl.pallas_call(finish_kernel, grid=(count // ROWS,), in_specs=[pl.BlockSp...  4.66 us
    unnamed x22, local copies, waits for them, and re-layouts  4.66 us
    ppermute x1, starting transfers between devices, local(): second = lax.ppermute(packs[1], 'fsdp', along_x(2))  4.64 us
    ppermute x1, starting transfers between devices, local(): lax.ppermute(packs[2], 'fsdp', along_x(3))  4.27 us
  transfers between devices with their start and end apart: 10, of which 3 were waited for; matrix products, arithmetic and copies ran while one was open for 0% of the time, Pallas kernels for 13%

profile of v3, /device:TPU:41, one launch (start us, length us, event | category | flops | bytes accessed | tf_op | source)
XLA Modules:
  0.0 109.2 jit_solution(4688588086639962101)
XLA Ops:
  7.2 0.0 all-gather.3.cloned.1.call-start
  7.2 0.7 all-gather.3.cloned.1.call-update
  7.9 3.4 %norm.1 = (f32[256,128]{1,0:T(8,128)}, bf16[256,1024]{1,0:T(8,128)(2,1)}, bf16[256,1536]{1,0:T(8,128)(2,1)}, bf16[256,1536]{1,0:T(8,128)(2,1)}, bf16[256,1536]{1,0:T(8,128)(2,1)}) custom-call(bf16[256,4096]{1,0:T(8,128)(2,1)} %tokens.3, bf16[256,512]{1,0:T(8,128)(2,1)} %refs_3_.1, f32[1,4096]{1,0:T(1,128)} %bitcast.11), custom_call_target="tpu_custom_call" | custom-call | flops 1 | bytes 1 | tf_op jit(solution)/shard_map/norm/pallas_call | solution.py:64
  11.3 4.6 %collective-permute-start = (bf16[256,1536]{1,0:T(8,128)(2,1)}, bf16[256,1536]{1,0:T(8,128)(2,1)S(1)}, u32[]{:S(2)}, u32[]{:S(2)}) collective-permute-start(bf16[256,1536]{1,0:T(8,128)(2,1)} %get-tuple-element.24), channel_id=1, source_target_pairs={{0,8},{1,9},{2,10},{3,11},{4,12},{5,13},{6,14},{7,15},{8,0},{9,1},... | collective-permute-start | bytes 2359304 | tf_op jit(solution)/shard_map/ppermute | solution.py:251
  16.0 16.4 %all-to-all-start = ((bf16[32,8,512]{2,1,0:T(8,128)(2,1)}), bf16[32,8,512]{2,1,0:T(8,128)(2,1)S(1)}, u32[]{:S(2)}, u32[]{:S(2)}) async-start(bf16[32,8,512]{2,1,0:T(8,128)(2,1)} %bitcast.1), calls=%async_computation | async-start | bytes 524288 | tf_op jit(solution)/shard_map/all_to_all | solution.py:246
  32.4 2.2 %collective-permute-start.1 = (bf16[256,1536]{1,0:T(8,128)(2,1)}, bf16[256,1536]{1,0:T(8,128)(2,1)S(1)}, u32[]{:S(2)}, u32[]{:S(2)}) collective-permute-start(bf16[256,1536]{1,0:T(8,128)(2,1)} %get-tuple-element.29), channel_id=1, source_target_pairs={{0,4},{1,5},{2,6},{3,7},{4,8},{5,9},{6,10},{7,11},{8,12},{9,13},{1... | collective-permute-start | bytes 2359304 | tf_op jit(solution)/shard_map/ppermute | solution.py:252
  34.7 4.3 %collective-permute-start.2 = (bf16[256,1536]{1,0:T(8,128)(2,1)}, bf16[256,1536]{1,0:T(8,128)(2,1)S(1)}, u32[]{:S(2)}, u32[]{:S(2)}) collective-permute-start(bf16[256,1536]{1,0:T(8,128)(2,1)} %get-tuple-element.30), channel_id=1, source_target_pairs={{0,12},{1,13},{2,14},{3,15},{4,0},{5,1},{6,2},{7,3},{8,4},{9,5},{1... | collective-permute-start | bytes 2359304 | tf_op jit(solution)/shard_map/ppermute | solution.py:252
  39.0 9.9 %all-to-all-done = bf16[32,8,512]{2,1,0:T(8,128)(2,1)S(1)} async-done(((bf16[32,8,512]{2,1,0:T(8,128)(2,1)}), bf16[32,8,512]{2,1,0:T(8,128)(2,1)S(1)}, u32[]{:S(2)}, u32[]{:S(2)}) %all-to-all-start) | async-done | bytes 262176 | tf_op jit(solution)/shard_map/all_to_all | solution.py:246
  48.9 0.0 collective-permute-done.refs_1_.refs_5_.refs_0_
  48.9 0.0 copy-start.5
  48.9 0.9 copy-done.5
  49.8 0.9 outer.1
  50.7 0.7 copy-done.4
  51.4 9.8 %all-to-all-start.1 = ((bf16[32,8,512]{2,1,0:T(8,128)(2,1)}), bf16[32,8,512]{2,1,0:T(8,128)(2,1)S(1)}, u32[]{:S(2)}, u32[]{:S(2)}) async-start(bf16[32,8,512]{2,1,0:T(8,128)(2,1)} %bitcast.9), calls=%async_computation.2 | async-start | bytes 524288 | tf_op jit(solution)/shard_map/all_to_all | solution.py:246
  61.2 0.0 reduce-scatter.2.cloned.1.call-start
  61.2 0.0 collective-permute-done.1.refs_2_.refs_6_
  61.3 0.0 collective-permute-done.2.refs_3_.refs_7_.refs_1_
  61.3 2.6 %partial.1 = bf16[1024,512]{1,0:T(8,128)(2,1)} custom-call(bf16[256,1024]{1,0:T(8,128)(2,1)S(1)} %copy-done.2, bf16[256,1536]{1,0:T(8,128)(2,1)S(1)} %collective-permute-done.refs_1_.refs_5_.refs_0_, bf16[256,1536]{1,0:T(8,128)(2,1)S(1)} %collective-permute-done.1.refs_2_.refs_6_, bf16[256,1536]{1,0:T(8,128)(2,1)S(1)} %collective-permute-done.2.refs_3_.refs_7_.refs_1_, ...), custom_call_target="tpu_custom_call" | custom-call | flops 1 | bytes 1 | tf_op jit(solution)/shard_map/partial/pallas_call | solution.py:124
  63.8 0.0 reduce-scatter.2.cloned.1.call-update
  63.9 0.0 all-gather.3.cloned.1.call-done
  63.9 1.2 %copy-done.1 = bf16[1,1024,512]{2,1,0:T(8,128)(2,1)S(1)} copy-done((bf16[1,1024,512]{2,1,0:T(8,128)(2,1)S(1)}, bf16[1,1024,512]{2,1,0:T(8,128)(2,1)}, u32[]{:S(2)}) %copy-start.1) | copy-done | bytes 1048600
  65.1 2.1 %back.1 = (bf16[256,1024]{1,0:T(8,128)(2,1)}, bf16[256,1024]{1,0:T(8,128)(2,1)}, bf16[256,1024]{1,0:T(8,128)(2,1)S(1)}, bf16[256,1024]{1,0:T(8,128)(2,1)S(1)}) custom-call(bf16[256,1536]{1,0:T(8,128)(2,1)S(1)} %collective-permute-done.refs_1_.refs_5_.refs_0_, bf16[256,1536]{1,0:T(8,128)(2,1)S(1)} %collective-permute-done.2.refs_3_.refs_7_.refs_1_, ...), custom_call_target="tpu_custom_call" | custom-call | flops 1 | bytes 1 | tf_op jit(solution)/shard_map/back/pallas_call | solution.py:94
  67.2 0.8 copy-done.3
  68.0 1.9 %collective-permute-start.3 = (bf16[256,1024]{1,0:T(8,128)(2,1)}, bf16[256,1024]{1,0:T(8,128)(2,1)S(1)}, u32[]{:S(2)}, u32[]{:S(2)}) collective-permute-start(bf16[256,1024]{1,0:T(8,128)(2,1)} %get-tuple-element.34), channel_id=1, source_target_pairs={{0,8},{1,9},{2,10},{3,11},{4,12},{5,13},{6,14},{7,15},{8,0},{9,1},... | collective-permute-start | bytes 1572872 | tf_op jit(solution)/shard_map/ppermute | solution.py:263
  70.0 3.4 %collective-permute-start.4 = (bf16[256,1024]{1,0:T(8,128)(2,1)}, bf16[256,1024]{1,0:T(8,128)(2,1)S(1)}, u32[]{:S(2)}, u32[]{:S(2)}) collective-permute-start(bf16[256,1024]{1,0:T(8,128)(2,1)} %get-tuple-element.35), channel_id=1, source_target_pairs={{0,4},{1,5},{2,6},{3,7},{4,8},{5,9},{6,10},{7,11},{8,12},{9,13},{1... | collective-permute-start | bytes 1572872 | tf_op jit(solution)/shard_map/ppermute | solution.py:264
  73.4 3.3 %collective-permute-start.5 = (bf16[256,1024]{1,0:T(8,128)(2,1)S(1)}, bf16[256,1024]{1,0:T(8,128)(2,1)S(1)}, u32[]{:S(2)}, u32[]{:S(2)}) collective-permute-start(bf16[256,1024]{1,0:T(8,128)(2,1)S(1)} %get-tuple-element.36), channel_id=1, source_target_pairs={{0,12},{1,13},{2,14},{3,15},{4,0},{5,1},{6,2},{7,3},{8,4},{9,5},{1... | collective-permute-start | bytes 1572872 | tf_op jit(solution)/shard_map/ppermute | solution.py:264
  76.7 0.7 place.1
  77.4 7.4 %collective-permute-done.3.refs_0_ = bf16[256,1024]{1,0:T(8,128)(2,1)S(1)} collective-permute-done((bf16[256,1024]{1,0:T(8,128)(2,1)}, bf16[256,1024]{1,0:T(8,128)(2,1)S(1)}, u32[]{:S(2)}, u32[]{:S(2)}) %collective-permute-start.3) | collective-permute-done | bytes 524320 | tf_op jit(solution)/shard_map/ppermute | solution.py:263
  84.8 11.9 %collective-permute-done.4.refs_1_ = bf16[256,1024]{1,0:T(8,128)(2,1)S(1)} collective-permute-done((bf16[256,1024]{1,0:T(8,128)(2,1)}, bf16[256,1024]{1,0:T(8,128)(2,1)S(1)}, u32[]{:S(2)}, u32[]{:S(2)}) %collective-permute-start.4) | collective-permute-done | bytes 524320 | tf_op jit(solution)/shard_map/ppermute | solution.py:264
  96.7 0.8 copy-done.9
  97.5 0.2 copy-done.10
  97.7 4.7 %finish.1 = bf16[256,4096]{1,0:T(8,128)(2,1)} custom-call(bf16[256,4096]{1,0:T(8,128)(2,1)} %tokens.3, f32[1,4096]{1,0:T(1,128)} %bitcast.12, f32[256,128]{1,0:T(8,128)} %get-tuple-element.32.inv_in, bf16[256,1024]{1,0:T(8,128)(2,1)} %copy-done.8, bf16[256,1024]{1,0:T(8,128)(2,1)} %copy-done.9, bf16[256,1024]{1,0:T(8,128)(2,1)} %copy-done.10, ...), custom_call_target="tpu_custom_call" | custom-call | flops 1 | bytes 1 | tf_op jit(solution)/shard_map/finish/pallas_call | solution.py:157
  (18 shorter events, 0.0 us)
Async XLA Ops:
  7.2 41.7 %copy-start.6 = (f32[8,512]{1,0:T(8,128)S(1)}, f32[8,512]{1,0:T(8,128)}, u32[]{:S(2)}) copy-start(f32[8,512]{1,0:T(8,128)} %master.1) | copy-start | bytes 49156
  7.2 41.7 %copy-start.7 = (f32[8,512]{1,0:T(8,128)S(1)}, f32[8,512]{1,0:T(8,128)}, u32[]{:S(2)}) copy-start(f32[8,512]{1,0:T(8,128)} %moment.1) | copy-start | bytes 49156
  7.2 56.7 %all-gather.3.cloned.1.call-start = ((), (), s32[]{:S(2)}) async-start(), calls=%async_computation.4 | async-start | bytes 1310720 | tf_op jit(solution)/shard_map/all_gather | solution.py:249
  11.3 37.5 %collective-permute-start = (bf16[256,1536]{1,0:T(8,128)(2,1)}, bf16[256,1536]{1,0:T(8,128)(2,1)S(1)}, u32[]{:S(2)}, u32[]{:S(2)}) collective-permute-start(bf16[256,1536]{1,0:T(8,128)(2,1)} %get-tuple-element.24), channel_id=1, source_target_pairs={{0,8},{1,9},{2,10},{3,11},{4,12},{5,13},{6,14},{7,15},{8,0},{9,1},... | collective-permute-start | bytes 2359304 | tf_op jit(solution)/shard_map/ppermute | solution.py:251
  16.0 32.9 %all-to-all-start = ((bf16[32,8,512]{2,1,0:T(8,128)(2,1)}), bf16[32,8,512]{2,1,0:T(8,128)(2,1)S(1)}, u32[]{:S(2)}, u32[]{:S(2)}) async-start(bf16[32,8,512]{2,1,0:T(8,128)(2,1)} %bitcast.1), calls=%async_computation | async-start | bytes 524288 | tf_op jit(solution)/shard_map/all_to_all | solution.py:246
  32.4 28.8 %collective-permute-start.1 = (bf16[256,1536]{1,0:T(8,128)(2,1)}, bf16[256,1536]{1,0:T(8,128)(2,1)S(1)}, u32[]{:S(2)}, u32[]{:S(2)}) collective-permute-start(bf16[256,1536]{1,0:T(8,128)(2,1)} %get-tuple-element.29), channel_id=1, source_target_pairs={{0,4},{1,5},{2,6},{3,7},{4,8},{5,9},{6,10},{7,11},{8,12},{9,13},{1... | collective-permute-start | bytes 2359304 | tf_op jit(solution)/shard_map/ppermute | solution.py:252
  34.7 26.6 %collective-permute-start.2 = (bf16[256,1536]{1,0:T(8,128)(2,1)}, bf16[256,1536]{1,0:T(8,128)(2,1)S(1)}, u32[]{:S(2)}, u32[]{:S(2)}) collective-permute-start(bf16[256,1536]{1,0:T(8,128)(2,1)} %get-tuple-element.30), channel_id=1, source_target_pairs={{0,12},{1,13},{2,14},{3,15},{4,0},{5,1},{6,2},{7,3},{8,4},{9,5},{1... | collective-permute-start | bytes 2359304 | tf_op jit(solution)/shard_map/ppermute | solution.py:252
  48.9 1.0 copy-start.5
  49.8 11.4 %copy-start = (bf16[256,512]{1,0:T(8,128)(2,1)S(1)}, bf16[256,512]{1,0:T(8,128)(2,1)}, u32[]{:S(2)}) copy-start(bf16[256,512]{1,0:T(8,128)(2,1)} %refs_3_.1) | copy-start | bytes 786436
  49.8 11.4 %copy-start.2 = (bf16[256,1024]{1,0:T(8,128)(2,1)S(1)}, bf16[256,1024]{1,0:T(8,128)(2,1)}, u32[]{:S(2)}) copy-start(bf16[256,1024]{1,0:T(8,128)(2,1)} %get-tuple-element.27.refs_0_) | copy-start | bytes 1572868
  50.7 0.7 copy-start.4
  51.4 25.3 %all-to-all-start.1 = ((bf16[32,8,512]{2,1,0:T(8,128)(2,1)}), bf16[32,8,512]{2,1,0:T(8,128)(2,1)S(1)}, u32[]{:S(2)}, u32[]{:S(2)}) async-start(bf16[32,8,512]{2,1,0:T(8,128)(2,1)} %bitcast.9), calls=%async_computation.2 | async-start | bytes 524288 | tf_op jit(solution)/shard_map/all_to_all | solution.py:246
  61.2 41.2 %reduce-scatter.2.cloned.1.call-start = ((), (), s32[]{:S(2)}) async-start(), calls=%async_computation.3 | async-start | bytes 1310720 | tf_op jit(solution)/shard_map/reduce_scatter | solution.py:260
  63.9 1.2 %copy-start.1 = (bf16[1,1024,512]{2,1,0:T(8,128)(2,1)S(1)}, bf16[1,1024,512]{2,1,0:T(8,128)(2,1)}, u32[]{:S(2)}) copy-start(bf16[1,1024,512]{2,1,0:T(8,128)(2,1)} %all-gather.3.cloned.1.call-done) | copy-start | bytes 3145732
  67.2 0.8 copy-start.3
  68.0 16.8 %collective-permute-start.3 = (bf16[256,1024]{1,0:T(8,128)(2,1)}, bf16[256,1024]{1,0:T(8,128)(2,1)S(1)}, u32[]{:S(2)}, u32[]{:S(2)}) collective-permute-start(bf16[256,1024]{1,0:T(8,128)(2,1)} %get-tuple-element.34), channel_id=1, source_target_pairs={{0,8},{1,9},{2,10},{3,11},{4,12},{5,13},{6,14},{7,15},{8,0},{9,1},... | collective-permute-start | bytes 1572872 | tf_op jit(solution)/shard_map/ppermute | solution.py:263
  70.0 26.8 %collective-permute-start.4 = (bf16[256,1024]{1,0:T(8,128)(2,1)}, bf16[256,1024]{1,0:T(8,128)(2,1)S(1)}, u32[]{:S(2)}, u32[]{:S(2)}) collective-permute-start(bf16[256,1024]{1,0:T(8,128)(2,1)} %get-tuple-element.35), channel_id=1, source_target_pairs={{0,4},{1,5},{2,6},{3,7},{4,8},{5,9},{6,10},{7,11},{8,12},{9,13},{1... | collective-permute-start | bytes 1572872 | tf_op jit(solution)/shard_map/ppermute | solution.py:264
  73.4 23.4 %collective-permute-start.5 = (bf16[256,1024]{1,0:T(8,128)(2,1)S(1)}, bf16[256,1024]{1,0:T(8,128)(2,1)S(1)}, u32[]{:S(2)}, u32[]{:S(2)}) collective-permute-start(bf16[256,1024]{1,0:T(8,128)(2,1)S(1)} %get-tuple-element.36), channel_id=1, source_target_pairs={{0,12},{1,13},{2,14},{3,15},{4,0},{5,1},{6,2},{7,3},{8,4},{9,5},{1... | collective-permute-start | bytes 1572872 | tf_op jit(solution)/shard_map/ppermute | solution.py:264
  84.8 11.9 %copy-start.8 = (bf16[256,1024]{1,0:T(8,128)(2,1)}, bf16[256,1024]{1,0:T(8,128)(2,1)S(1)}, u32[]{:S(2)}) copy-start(bf16[256,1024]{1,0:T(8,128)(2,1)S(1)} %collective-permute-done.3.refs_0_) | copy-start | bytes 1572868
  96.7 0.8 copy-start.9
  96.7 1.0 copy-start.10
Sparse Core Ops, SparseCore 0:
  10.1 43.8 all-gather.2
  65.4 30.6 reduce-scatter.1
